TPU v7x, 32 devices: a whole 2x2x4 slice. The times are simulated.
32 devices in a mesh: bx: 8 (over z, y), by: 4 (over x, core).
Axes of the slice: x: 2, y: 2, z: 4, core: 2. Of those that a mesh axis runs over, the one named last changes fastest.
Arguments:
- views: bfloat16 [4, 512, 256, 128], P(None, ('bx', 'by')), may hold values from 0.25 to 4
- offsets: int32 [4, 2], replicated, may hold values from -16 to 16, as said below
- background: float32 [4], replicated, may hold values from 0.5 to 2
- psf_x: float32 [4, 9], replicated, may hold values from 0.1 to 1
- psf_y: float32 [4, 9], replicated, may hold values from 0.1 to 1
- psf_z: float32 [4, 21], replicated, may hold values from 0.1 to 1
- start: float32 [512, 256, 128], P('bx', 'by'), may hold values from 0.5 to 2
Outputs:
- estimate: float32 [512, 256, 128], P('bx', 'by')
Inputs may be any that keep to these rules, and one draw needn't show every extreme that they name: Every offset is nonzero; view 0 has offsets (-16, -16), view 3 has (16, 16), view 1 has a positive first and a negative second offset, view 2 the reverse.
All inputs are finite; a program needn't handle non-finite values.
Results may differ from a plain program's by a relative error of at most 0.0003.
Values may be sent and summed in bfloat16 or wider, within the bound.
A program may use at most 128 MiB of HBM per device.

v0:
```python
import jax
import jax.numpy as jnp
from jax import lax
from jax.sharding import PartitionSpec as P

V = 4
SHIFT = 16
ITERS = 2


def padded_2(cells, sides, width):
    for axis, dim in sides:
        count = lax.axis_size(axis)
        ends = count - 1
        head = lax.slice_in_dim(cells, 0, width, axis=dim)
        tail = lax.slice_in_dim(cells, cells.shape[dim] - width, cells.shape[dim], axis=dim)
        cells = jnp.concatenate(
            [
                lax.ppermute(tail, axis, [(i, (i + 1) % count) for i in range(ends)]),
                cells,
                lax.ppermute(head, axis, [((i + 1) % count, i) for i in range(ends)]),
            ],
            axis=dim,
        )
    return cells


def band_rows(tap_row, extent):
    length = tap_row.shape[0]
    distance = jnp.arange(extent + length - 1)[None, :] - jnp.arange(extent)[:, None]
    picked = distance[:, :, None] == jnp.arange(length)[None, None, :]
    return jnp.sum(jnp.where(picked, tap_row[None, None, :], 0.0), axis=2)


def depth_band(tap_row, extent):
    length = tap_row.shape[0]
    middle = (length - 1) // 2
    distance = jnp.arange(extent)[:, None] - jnp.arange(extent)[None, :] + middle
    picked = distance[:, :, None] == jnp.arange(length)[None, None, :]
    return jnp.sum(jnp.where(picked, tap_row[None, None, :], 0.0), axis=2)


def blur_local(field, taps_x, taps_y, taps_z):
    middle = (taps_x.shape[0] - 1) // 2
    rows_out = field.shape[0] - 2 * middle
    cols_out = field.shape[1] - 2 * middle
    first = jnp.einsum(
        "ij,jyz->iyz", band_rows(taps_x, rows_out), field, precision=lax.Precision.HIGHEST
    )
    second = jnp.einsum(
        "ij,xjz->xiz", band_rows(taps_y, cols_out), first, precision=lax.Precision.HIGHEST
    )
    return jnp.einsum(
        "xyj,ji->xyi", second, depth_band(taps_z, field.shape[2]), precision=lax.Precision.HIGHEST
    )


def local(views, offsets, background, psf_x, psf_y, psf_z, start):
    rows_x, rows_y, depth = start.shape
    full_x = rows_x * lax.axis_size("bx")
    full_y = rows_y * lax.axis_size("by")
    middle = (psf_x.shape[1] - 1) // 2
    routed = lax.all_to_all(views, "by", split_axis=2, concat_axis=1, tiled=True)
    margin = 0
    padded = padded_2(routed, (("bx", 1), ("by", 2)), SHIFT + margin)
    base_x = (
        lax.axis_index("bx") * rows_x - middle + jnp.arange(rows_x + 2 * middle, dtype=jnp.int32)
    )
    base_y = (
        lax.axis_index("by") * rows_y - middle + jnp.arange(rows_y + 2 * middle, dtype=jnp.int32)
    )
    inside_x = ((base_x >= 0) & (base_x < full_x)).astype(jnp.float32)
    inside_y = ((base_y >= 0) & (base_y < full_y)).astype(jnp.float32)
    weight = jnp.zeros(start.shape, jnp.float32)
    kernels = []
    planes = []
    registered = []
    for which in range(V):
        taps_x = psf_x[which] / jnp.sum(psf_x[which])
        taps_y = psf_y[which] / jnp.sum(psf_y[which])
        taps_z = psf_z[which] / jnp.sum(psf_z[which])
        kernels.append((taps_x, taps_y, taps_z))
        shift_x = offsets[which, 0]
        shift_y = offsets[which, 1]
        cover_x = ((base_x + shift_x >= 0) & (base_x + shift_x < full_x)).astype(
            jnp.float32
        ) * inside_x
        cover_y = ((base_y + shift_y >= 0) & (base_y + shift_y < full_y)).astype(
            jnp.float32
        ) * inside_y
        planes.append(cover_x[:, None] * cover_y[None, :])
        weight_x = jnp.dot(
            band_rows(taps_x[::-1], rows_x), cover_x, precision=lax.Precision.HIGHEST
        )
        weight_y = jnp.dot(
            band_rows(taps_y[::-1], rows_y), cover_y, precision=lax.Precision.HIGHEST
        )
        weight_z = jnp.sum(depth_band(taps_z[::-1], depth), axis=0)
        weight = (
            weight + weight_x[:, None, None] * weight_y[None, :, None] * weight_z[None, None, :]
        )
        registered.append(
            lax.dynamic_slice(
                padded[which],
                (SHIFT + shift_x, SHIFT + shift_y, jnp.zeros((), jnp.int32)),
                (rows_x + 2 * margin, rows_y + 2 * margin, depth),
            )
        )
    estimate = start
    for sweep in range(ITERS):
        padded_est = padded_2(
            estimate.astype(jnp.bfloat16), (("bx", 0), ("by", 1)), middle + margin
        ).astype(estimate.dtype)
        summed = jnp.zeros(start.shape, jnp.float32)
        stacked = jnp.stack(
            [
                registered[which].astype(jnp.float32)
                / (
                    blur_local(padded_est, kernels[which][0], kernels[which][1], kernels[which][2])
                    + background[which]
                )
                for which in range(V)
            ]
        )
        rims = padded_2(stacked.astype(jnp.bfloat16), (("bx", 1), ("by", 2)), middle).astype(
            stacked.dtype
        )
        for which in range(V):
            taps_x, taps_y, taps_z = kernels[which]
            summed = summed + blur_local(rims[which], taps_x[::-1], taps_y[::-1], taps_z[::-1])
        estimate = estimate * summed / weight
    return estimate


def solution(mesh):
    return jax.shard_map(
        local,
        mesh=mesh,
        in_specs=(P(None, ("bx", "by"), None, None), P(), P(), P(), P(), P(), P("bx", "by", None)),
        out_specs=P("bx", "by", None),
        check_vma=False,
    )
```

profile of v0, /device:TPU:5, one launch (start us, length us, event | category | flops | bytes accessed | tf_op | source)
XLA Modules:
  0.0 349.1 jit_solution(14171809431439997482)
XLA Ops:
  0.0 2.8 copy.99
  2.9 3.1 collective-permute-start.4
  8.2 6.9 %copy.11 = bf16[4,16,256,128]{3,1,0,2:T(8,128)(2,1)} copy(bf16[4,16,256,128]{3,2,1,0:T(8,128)(2,1)} %param.7) | data formatting | bytes 8388608 | tf_op args[0]
  15.0 6.2 %all-to-all-start = ((bf16[4,16,256,128]{3,1,0,2:T(8,128)(2,1)}), bf16[4,16,256,128]{3,1,0,2:T(8,128)(2,1)}, u32[]{:S(2)}, u32[]{:S(2)}) async-start(bf16[4,16,256,128]{3,1,0,2:T(8,128)(2,1)} %copy.11), calls=%async_computation | async-start | bytes 8388608 | tf_op jit(solution)/shard_map/all_to_all | solution.py:63
  38.6 3.2 broadcast_divide_fusion.21
  59.7 8.9 %all-to-all-done = bf16[4,16,256,128]{3,1,0,2:T(8,128)(2,1)} async-done(((bf16[4,16,256,128]{3,1,0,2:T(8,128)(2,1)}), bf16[4,16,256,128]{3,1,0,2:T(8,128)(2,1)}, u32[]{:S(2)}, u32[]{:S(2)}) %all-to-all-start) | async-done | bytes 4194336 | tf_op jit(solution)/shard_map/all_to_all | solution.py:63
  68.6 4.9 %copy.12 = bf16[4,16,4,64,128]{4,3,1,2,0:T(8,128)(2,1)S(1)} copy(bf16[4,16,4,64,128]{4,1,0,3,2:T(8,128)(2,1)} %bitcast.2) | data formatting | bytes 8388608 | tf_op jit(solution)/shard_map/all_to_all | solution.py:63
  73.7 4.0 %collective-permute-start = (bf16[4,16,64,128]{3,2,1,0:T(8,128)(2,1)S(1)}, bf16[4,16,64,128]{3,2,1,0:T(8,128)(2,1)S(1)}, u32[]{:S(2)}, u32[]{:S(2)}) collective-permute-start(bf16[4,16,64,128]{3,2,1,0:T(8,128)(2,1)S(1)} %get-tuple-element.73), channel_id=1, source_target_pairs={{0,4},{4,8},{8,12},{12,16},{16,20},{20,24},{24,28},{1,5},{5,9},{9,... | collective-permute-start | bytes 3145736 | tf_op jit(solution)/shard_map/ppermute | solution.py:19
  79.8 3.0 collective-permute-start.6
  85.7 3.1 collective-permute-done.7
  92.7 29.2 %collective-permute-done = bf16[4,16,64,128]{3,2,1,0:T(8,128)(2,1)S(1)} collective-permute-done((bf16[4,16,64,128]{3,2,1,0:T(8,128)(2,1)S(1)}, bf16[4,16,64,128]{3,2,1,0:T(8,128)(2,1)S(1)}, u32[]{:S(2)}, u32[]{:S(2)}) %collective-permute-start) | collective-permute-done | bytes 1048608 | tf_op jit(solution)/shard_map/ppermute | solution.py:19
  122.7 3.9 %collective-permute-start.2 = (bf16[4,96,16,128]{3,2,1,0:T(8,128)(2,1)S(1)}, bf16[4,96,16,128]{3,2,1,0:T(8,128)(2,1)S(1)}, u32[]{:S(2)}, u32[]{:S(2)}) collective-permute-start(bf16[4,96,16,128]{3,2,1,0:T(8,128)(2,1)S(1)} %get-tuple-element.55), channel_id=1, source_target_pairs={{0,1},{1,2},{2,3},{4,5},{5,6},{6,7},{8,9},{9,10},{10,11},{12,13},{... | collective-permute-start | bytes 4718600 | tf_op jit(solution)/shard_map/ppermute | solution.py:19
  129.8 3.5 fusion.30
  133.2 3.5 fusion.28
  136.7 3.5 fusion.26
  140.2 3.5 fusion.24
  144.0 4.4 %collective-permute-done.3 = bf16[4,96,16,128]{3,2,1,0:T(8,128)(2,1)S(1)} collective-permute-done((bf16[4,96,16,128]{3,2,1,0:T(8,128)(2,1)S(1)}, bf16[4,96,16,128]{3,2,1,0:T(8,128)(2,1)S(1)}, u32[]{:S(2)}, u32[]{:S(2)}) %collective-permute-start.3) | collective-permute-done | bytes 1572896 | tf_op jit(solution)/shard_map/ppermute | solution.py:21
  148.4 17.1 %pad_maximum_fusion = bf16[4,96,96,128]{3,2,1,0:T(8,128)(2,1)S(1)} fusion(bf16[4,96,16,128]{3,2,1,0:T(8,128)(2,1)S(1)} %collective-permute-done.3, bf16[4,16,64,128]{3,2,1,0:T(8,128)(2,1)S(1)} %collective-permute-done.1, bf16[4,64,64,128]{3,2,1,0:T(8,128)(2,1)S(1)} %bitcast.370, bf16[4,16,64,128]{3,2,1,0:T(8,128)(2,1)S(1)} %collective-permute-done, ...), kind=kLoop, calls=%fused_computation | loop fusion | flops 47185920 | bytes 18874368 | tf_op jit(solution)/shard_map/concatenate | solution.py:17
  167.7 2.8 fusion.114
  173.1 2.7 fusion.102
  178.6 4.9 %collective-permute-start.8 = (bf16[4,4,64,128]{3,2,1,0:T(8,128)(2,1)S(1)}, bf16[4,4,64,128]{3,2,1,0:T(8,128)(2,1)S(1)}, u32[]{:S(2)}, u32[]{:S(2)}) collective-permute-start(bf16[4,4,64,128]{3,2,1,0:T(8,128)(2,1)S(1)} %get-tuple-element.71), channel_id=1, source_target_pairs={{0,4},{4,8},{8,12},{12,16},{16,20},{20,24},{24,28},{1,5},{5,9},{9,... | collective-permute-start | bytes 786440 | tf_op jit(solution)/shard_map/ppermute | solution.py:19
  188.5 3.0 collective-permute-done.9
  191.8 3.2 collective-permute-start.10
  198.6 4.4 %collective-permute-done.11 = bf16[4,72,4,128]{3,2,1,0:T(4,128)(2,1)S(1)} collective-permute-done((bf16[4,72,4,128]{3,2,1,0:T(4,128)(2,1)S(1)}, bf16[4,72,4,128]{3,2,1,0:T(4,128)(2,1)S(1)}, u32[]{:S(2)}, u32[]{:S(2)}) %collective-permute-start.11) | collective-permute-done | bytes 294944 | tf_op jit(solution)/shard_map/ppermute | solution.py:21
  203.0 7.4 %pad_maximum_fusion.1 = bf16[4,72,72,128]{3,2,1,0:T(8,128)(2,1)S(1)} fusion(bf16[4,72,4,128]{3,2,1,0:T(4,128)(2,1)S(1)} %collective-permute-done.11, bf16[4,4,64,128]{3,2,1,0:T(8,128)(2,1)S(1)} %collective-permute-done.9, bf16[1,64,64,128]{3,2,1,0:T(8,128)(2,1)S(1)} %fusion.96, bf16[1,64,64,128]{3,2,1,0:T(8,128)(2,1)S(1)} %fusion.102, ...), kind=kLoop, calls=%fused_computation.1 | loop fusion | flops 42467328 | bytes 10616832 | tf_op jit(solution)/shard_map/concatenate | solution.py:17
  212.4 3.4 fusion.18
  217.0 3.5 fusion.20
  221.6 3.6 %fusion.16 = f32[64,128,64]{1,2,0:T(8,128)S(1)} fusion(f32[64,72,128]{2,0,1:T(8,128)S(1)} %fusion.125, f32[64,72]{1,0:T(8,128)S(1)} %get-tuple-element.24), kind=kOutput, calls=%fused_computation.27 | convolution fusion | flops 452984832 | bytes 4474880 | tf_op jit(solution)/shard_map/ij,xjz->xiz/dot_general | solution.py:50
  226.3 3.4 fusion.22
  236.0 3.3 fusion.279
  239.3 3.5 collective-permute-start.12
  245.1 3.5 %collective-permute-done.13 = bf16[4,64,128]{2,1,0:T(8,128)(2,1)S(1)} collective-permute-done((bf16[4,64,128]{2,1,0:T(8,128)(2,1)S(1)}, bf16[4,64,128]{2,1,0:T(8,128)(2,1)S(1)}, u32[]{:S(2)}, u32[]{:S(2)}) %collective-permute-start.13) | collective-permute-done | bytes 65568 | tf_op jit(solution)/shard_map/ppermute | solution.py:21
  248.7 3.2 collective-permute-start.14
  253.8 3.7 %collective-permute-done.15 = bf16[72,4,128]{2,1,0:T(4,128)(2,1)S(1)} collective-permute-done((bf16[72,4,128]{2,1,0:T(4,128)(2,1)S(1)}, bf16[72,4,128]{2,1,0:T(4,128)(2,1)S(1)}, u32[]{:S(2)}, u32[]{:S(2)}) %collective-permute-start.15) | collective-permute-done | bytes 73760 | tf_op jit(solution)/shard_map/ppermute | solution.py:21
  262.8 3.5 fusion.14
  266.3 2.7 fusion.111
  269.0 3.6 %fusion.12 = f32[64,128,64]{1,2,0:T(8,128)S(1)} fusion(f32[64,72,128]{2,0,1:T(8,128)S(1)} %fusion.137, f32[64,72]{1,0:T(8,128)S(1)} %get-tuple-element.34), kind=kOutput, calls=%fused_computation.23 | convolution fusion | flops 452984832 | bytes 4474880 | tf_op jit(solution)/shard_map/ij,xjz->xiz/dot_general | solution.py:50
  275.2 3.5 fusion.10
  281.4 3.9 %fusion.8 = f32[64,128,64]{1,2,0:T(8,128)S(1)} fusion(f32[64,72,128]{2,0,1:T(8,128)S(1)} %fusion.133, f32[64,72]{1,0:T(8,128)S(1)} %get-tuple-element.30), kind=kOutput, calls=%fused_computation.19 | convolution fusion | flops 452984832 | bytes 4474880 | tf_op jit(solution)/shard_map/ij,xjz->xiz/dot_general | solution.py:50
  289.9 3.4 collective-permute-start.17
  293.3 8.2 %collective-permute-done.16 = bf16[4,4,64,128]{3,2,1,0:T(8,128)(2,1)S(1)} collective-permute-done((bf16[4,4,64,128]{3,2,1,0:T(8,128)(2,1)S(1)}, bf16[4,4,64,128]{3,2,1,0:T(8,128)(2,1)S(1)}, u32[]{:S(2)}, u32[]{:S(2)}) %collective-permute-start.16) | collective-permute-done | bytes 262176 | tf_op jit(solution)/shard_map/ppermute | solution.py:19
  307.3 4.4 %collective-permute-done.19 = bf16[4,72,4,128]{3,2,1,0:T(4,128)(2,1)S(1)} collective-permute-done((bf16[4,72,4,128]{3,2,1,0:T(4,128)(2,1)S(1)}, bf16[4,72,4,128]{3,2,1,0:T(4,128)(2,1)S(1)}, u32[]{:S(2)}, u32[]{:S(2)}) %collective-permute-start.19) | collective-permute-done | bytes 294944 | tf_op jit(solution)/shard_map/ppermute | solution.py:21
  311.7 7.0 %pad_maximum_fusion.2 = bf16[4,72,72,128]{3,2,1,0:T(8,128)(2,1)S(1)} fusion(bf16[4,72,4,128]{3,2,1,0:T(4,128)(2,1)S(1)} %collective-permute-done.19, bf16[4,4,64,128]{3,2,1,0:T(8,128)(2,1)S(1)} %collective-permute-done.17, bf16[1,64,64,128]{3,2,1,0:T(8,128)(2,1)S(1)} %fusion.93, bf16[1,64,64,128]{3,2,1,0:T(8,128)(2,1)S(1)} %fusion.99, ...), kind=kLoop, calls=%fused_computation.2 | loop fusion | flops 42467328 | bytes 10616832 | tf_op jit(solution)/shard_map/concatenate | solution.py:17
  320.8 3.4 fusion.2
  327.2 3.5 fusion.4
  333.8 3.4 fusion
  340.2 3.4 fusion.6
  343.7 5.2 %multiply_divide_fusion = f32[64,64,128]{2,1,0:T(8,128)} fusion(f32[64,64,128]{2,1,0:T(8,128)S(1)} %get-tuple-element.120, f32[64,64,128]{2,1,0:T(8,128)S(1)} %fusion.40, f32[64,64,128]{2,1,0:T(8,128)S(1)} %fusion.42, f32[64,64,128]{2,1,0:T(8,128)S(1)} %fusion.44, f32[64,128,64]{1,2,0:T(8,128)S(1)} %fusion.6, f32[128]{0:T(128)S(1)} %copy-done.22, ...), kind=kOutput, calls=%fused_computation.84 | convolution fusion | flops 811597824 | bytes 12716032 | tf_op jit(solution)/shard_map/xyj,ji->xyi/dot_general | solution.py:53
  (153 shorter events, 104.6 us)
Async XLA Ops:
  2.9 76.8 %collective-permute-start.4 = (bf16[4,64,128]{2,0,1:T(4,128)(2,1)S(1)}, bf16[4,64,128]{2,0,1:T(4,128)(2,1)S(1)}, u32[]{:S(2)}, u32[]{:S(2)}) collective-permute-start(bf16[4,64,128]{2,0,1:T(4,128)(2,1)S(1)} %get-tuple-element.81), channel_id=1, source_target_pairs={{0,4},{4,8},{8,12},{12,16},{16,20},{20,24},{24,28},{1,5},{5,9},{9,... | collective-permute-start | bytes 196616 | tf_op jit(solution)/shard_map/ppermute | solution.py:19
  6.0 73.7 %collective-permute-start.5 = (bf16[4,64,128]{2,0,1:T(4,128)(2,1)S(1)}, bf16[4,64,128]{2,0,1:T(4,128)(2,1)S(1)}, u32[]{:S(2)}, u32[]{:S(2)}) collective-permute-start(bf16[4,64,128]{2,0,1:T(4,128)(2,1)S(1)} %get-tuple-element.82), channel_id=1, source_target_pairs={{4,0},{8,4},{12,8},{16,12},{20,16},{24,20},{28,24},{5,1},{9,5},{13... | collective-permute-start | bytes 196616 | tf_op jit(solution)/shard_map/ppermute | solution.py:21
  15.0 6.2 %copy-start.16 = (s32[4,2]{0,1:T(2,128)S(1)}, s32[4,2]{0,1:T(2,128)}, u32[]{:S(2)}) copy-start(s32[4,2]{0,1:T(2,128)} %param.8) | copy-start | bytes 100
  15.0 10.6 %copy-start.19 = (f32[4,9]{1,0:T(4,128)S(1)}, f32[4,9]{1,0:T(4,128)}, u32[]{:S(2)}) copy-start(f32[4,9]{1,0:T(4,128)} %param.11) | copy-start | bytes 436
  15.0 11.3 %copy-start.17 = (f32[4,9]{1,0:T(4,128)S(1)}, f32[4,9]{1,0:T(4,128)}, u32[]{:S(2)}) copy-start(f32[4,9]{1,0:T(4,128)} %param.10) | copy-start | bytes 436
  15.0 12.4 %copy-start.18 = (f32[4,21]{1,0:T(4,128)S(1)}, f32[4,21]{1,0:T(4,128)}, u32[]{:S(2)}) copy-start(f32[4,21]{1,0:T(4,128)} %param.12) | copy-start | bytes 1012
  15.0 53.6 %all-to-all-start = ((bf16[4,16,256,128]{3,1,0,2:T(8,128)(2,1)}), bf16[4,16,256,128]{3,1,0,2:T(8,128)(2,1)}, u32[]{:S(2)}, u32[]{:S(2)}) async-start(bf16[4,16,256,128]{3,1,0,2:T(8,128)(2,1)} %copy.11), calls=%async_computation | async-start | bytes 8388608 | tf_op jit(solution)/shard_map/all_to_all | solution.py:63
  45.2 43.6 %copy-start.7 = (f32[64,72]{1,0:T(8,128)}, f32[64,72]{1,0:T(8,128)S(1)}, u32[]{:S(2)}) copy-start(f32[64,72]{1,0:T(8,128)S(1)} %get-tuple-element.37) | copy-start | bytes 55300
  45.2 44.9 %copy-start.5 = (f32[64,72]{1,0:T(8,128)}, f32[64,72]{1,0:T(8,128)S(1)}, u32[]{:S(2)}) copy-start(f32[64,72]{1,0:T(8,128)S(1)} %get-tuple-element.35) | copy-start | bytes 55300
  45.2 46.3 %copy-start.3 = (f32[64,72]{1,0:T(8,128)}, f32[64,72]{1,0:T(8,128)S(1)}, u32[]{:S(2)}) copy-start(f32[64,72]{1,0:T(8,128)S(1)} %get-tuple-element.33) | copy-start | bytes 55300
  45.2 83.4 %copy-start.1 = (f32[64,72]{1,0:T(8,128)}, f32[64,72]{1,0:T(8,128)S(1)}, u32[]{:S(2)}) copy-start(f32[64,72]{1,0:T(8,128)S(1)} %get-tuple-element.31) | copy-start | bytes 55300
  73.5 11.5 %copy-start.20 = (f32[4]{0:T(128)S(1)}, f32[4]{0:T(128)}, u32[]{:S(2)}) copy-start(f32[4]{0:T(128)} %param.9) | copy-start | bytes 52
  73.7 48.2 %collective-permute-start = (bf16[4,16,64,128]{3,2,1,0:T(8,128)(2,1)S(1)}, bf16[4,16,64,128]{3,2,1,0:T(8,128)(2,1)S(1)}, u32[]{:S(2)}, u32[]{:S(2)}) collective-permute-start(bf16[4,16,64,128]{3,2,1,0:T(8,128)(2,1)S(1)} %get-tuple-element.73), channel_id=1, source_target_pairs={{0,4},{4,8},{8,12},{12,16},{16,20},{20,24},{24,28},{1,5},{5,9},{9,... | collective-permute-start | bytes 3145736 | tf_op jit(solution)/shard_map/ppermute | solution.py:19
  77.8 44.1 %collective-permute-start.1 = (bf16[4,16,64,128]{3,2,1,0:T(8,128)(2,1)S(1)}, bf16[4,16,64,128]{3,2,1,0:T(8,128)(2,1)S(1)}, u32[]{:S(2)}, u32[]{:S(2)}) collective-permute-start(bf16[4,16,64,128]{3,2,1,0:T(8,128)(2,1)S(1)} %get-tuple-element.74), channel_id=1, source_target_pairs={{4,0},{8,4},{12,8},{16,12},{20,16},{24,20},{28,24},{5,1},{9,5},{13... | collective-permute-start | bytes 3145736 | tf_op jit(solution)/shard_map/ppermute | solution.py:21
  79.8 5.9 %collective-permute-start.6 = (bf16[72,4,128]{2,0,1:T(8,128)(2,1)S(1)}, bf16[72,4,128]{2,0,1:T(8,128)(2,1)S(1)}, u32[]{:S(2)}, u32[]{:S(2)}) collective-permute-start(bf16[72,4,128]{2,0,1:T(8,128)(2,1)S(1)} %get-tuple-element.77), channel_id=1, source_target_pairs={{0,1},{1,2},{2,3},{4,5},{5,6},{6,7},{8,9},{9,10},{10,11},{12,13},{... | collective-permute-start | bytes 221192 | tf_op jit(solution)/shard_map/ppermute | solution.py:19
  82.8 6.0 %collective-permute-start.7 = (bf16[72,4,128]{2,0,1:T(8,128)(2,1)S(1)}, bf16[72,4,128]{2,0,1:T(8,128)(2,1)S(1)}, u32[]{:S(2)}, u32[]{:S(2)}) collective-permute-start(bf16[72,4,128]{2,0,1:T(8,128)(2,1)S(1)} %get-tuple-element.78), channel_id=1, source_target_pairs={{1,0},{2,1},{3,2},{5,4},{6,5},{7,6},{9,8},{10,9},{11,10},{13,12},{... | collective-permute-start | bytes 221192 | tf_op jit(solution)/shard_map/ppermute | solution.py:21
  122.7 21.3 %collective-permute-start.2 = (bf16[4,96,16,128]{3,2,1,0:T(8,128)(2,1)S(1)}, bf16[4,96,16,128]{3,2,1,0:T(8,128)(2,1)S(1)}, u32[]{:S(2)}, u32[]{:S(2)}) collective-permute-start(bf16[4,96,16,128]{3,2,1,0:T(8,128)(2,1)S(1)} %get-tuple-element.55), channel_id=1, source_target_pairs={{0,1},{1,2},{2,3},{4,5},{5,6},{6,7},{8,9},{9,10},{10,11},{12,13},{... | collective-permute-start | bytes 4718600 | tf_op jit(solution)/shard_map/ppermute | solution.py:19
  126.6 21.7 %collective-permute-start.3 = (bf16[4,96,16,128]{3,2,1,0:T(8,128)(2,1)S(1)}, bf16[4,96,16,128]{3,2,1,0:T(8,128)(2,1)S(1)}, u32[]{:S(2)}, u32[]{:S(2)}) collective-permute-start(bf16[4,96,16,128]{3,2,1,0:T(8,128)(2,1)S(1)} %get-tuple-element.56), channel_id=1, source_target_pairs={{1,0},{2,1},{3,2},{5,4},{6,5},{7,6},{9,8},{10,9},{11,10},{13,12},{... | collective-permute-start | bytes 4718600 | tf_op jit(solution)/shard_map/ppermute | solution.py:21
  165.5 2.2 copy-start.14
  167.7 2.8 copy-start.13
  170.5 2.6 copy-start.12
  173.1 2.8 copy-start.11
  178.5 7.7 %copy-start.23 = (f32[64]{0:T(128)S(1)}, f32[64]{0:T(128)}, u32[]{:S(2)}) copy-start(f32[64]{0:T(128)} %convolution_bitcast_fusion.3) | copy-start | bytes 772
  178.5 7.7 %copy-start.24 = (f32[64]{0:T(128)S(1)}, f32[64]{0:T(128)}, u32[]{:S(2)}) copy-start(f32[64]{0:T(128)} %convolution_bitcast_fusion.2) | copy-start | bytes 772
  178.6 9.9 %collective-permute-start.8 = (bf16[4,4,64,128]{3,2,1,0:T(8,128)(2,1)S(1)}, bf16[4,4,64,128]{3,2,1,0:T(8,128)(2,1)S(1)}, u32[]{:S(2)}, u32[]{:S(2)}) collective-permute-start(bf16[4,4,64,128]{3,2,1,0:T(8,128)(2,1)S(1)} %get-tuple-element.71), channel_id=1, source_target_pairs={{0,4},{4,8},{8,12},{12,16},{16,20},{20,24},{24,28},{1,5},{5,9},{9,... | collective-permute-start | bytes 786440 | tf_op jit(solution)/shard_map/ppermute | solution.py:19
  183.6 8.0 %collective-permute-start.9 = (bf16[4,4,64,128]{3,2,1,0:T(8,128)(2,1)S(1)}, bf16[4,4,64,128]{3,2,1,0:T(8,128)(2,1)S(1)}, u32[]{:S(2)}, u32[]{:S(2)}) collective-permute-start(bf16[4,4,64,128]{3,2,1,0:T(8,128)(2,1)S(1)} %get-tuple-element.72), channel_id=1, source_target_pairs={{4,0},{8,4},{12,8},{16,12},{20,16},{24,20},{28,24},{5,1},{9,5},{13... | collective-permute-start | bytes 786440 | tf_op jit(solution)/shard_map/ppermute | solution.py:21
  191.8 6.8 %collective-permute-start.10 = (bf16[4,72,4,128]{3,2,1,0:T(4,128)(2,1)S(1)}, bf16[4,72,4,128]{3,2,1,0:T(4,128)(2,1)S(1)}, u32[]{:S(2)}, u32[]{:S(2)}) collective-permute-start(bf16[4,72,4,128]{3,2,1,0:T(4,128)(2,1)S(1)} %get-tuple-element.67), channel_id=1, source_target_pairs={{0,1},{1,2},{2,3},{4,5},{5,6},{6,7},{8,9},{9,10},{10,11},{12,13},{... | collective-permute-start | bytes 884744 | tf_op jit(solution)/shard_map/ppermute | solution.py:19
  195.0 8.0 %collective-permute-start.11 = (bf16[4,72,4,128]{3,2,1,0:T(4,128)(2,1)S(1)}, bf16[4,72,4,128]{3,2,1,0:T(4,128)(2,1)S(1)}, u32[]{:S(2)}, u32[]{:S(2)}) collective-permute-start(bf16[4,72,4,128]{3,2,1,0:T(4,128)(2,1)S(1)} %get-tuple-element.68), channel_id=1, source_target_pairs={{1,0},{2,1},{3,2},{5,4},{6,5},{7,6},{9,8},{10,9},{11,10},{13,12},{... | collective-permute-start | bytes 884744 | tf_op jit(solution)/shard_map/ppermute | solution.py:21
  233.5 2.4 copy-start
  233.6 2.4 copy-start.9
  233.6 2.4 copy-start.10
  233.6 2.4 copy-start.21
  233.6 2.4 copy-start.22
  239.2 19.1 %copy-start.8 = (f32[64,72]{1,0:T(8,128)S(1)}, f32[64,72]{1,0:T(8,128)}, u32[]{:S(2)}) copy-start(f32[64,72]{1,0:T(8,128)} %copy-done.7) | copy-start | bytes 55300
  239.3 5.9 %collective-permute-start.12 = (bf16[4,64,128]{2,1,0:T(8,128)(2,1)S(1)}, bf16[4,64,128]{2,1,0:T(8,128)(2,1)S(1)}, u32[]{:S(2)}, u32[]{:S(2)}) collective-permute-start(bf16[4,64,128]{2,1,0:T(8,128)(2,1)S(1)} %get-tuple-element.79), channel_id=1, source_target_pairs={{0,4},{4,8},{8,12},{12,16},{16,20},{20,24},{24,28},{1,5},{5,9},{9,... | collective-permute-start | bytes 196616 | tf_op jit(solution)/shard_map/ppermute | solution.py:19
  242.7 5.9 %collective-permute-start.13 = (bf16[4,64,128]{2,1,0:T(8,128)(2,1)S(1)}, bf16[4,64,128]{2,1,0:T(8,128)(2,1)S(1)}, u32[]{:S(2)}, u32[]{:S(2)}) collective-permute-start(bf16[4,64,128]{2,1,0:T(8,128)(2,1)S(1)} %get-tuple-element.80), channel_id=1, source_target_pairs={{4,0},{8,4},{12,8},{16,12},{20,16},{24,20},{28,24},{5,1},{9,5},{13... | collective-permute-start | bytes 196616 | tf_op jit(solution)/shard_map/ppermute | solution.py:21
  248.7 5.1 %collective-permute-start.14 = (bf16[72,4,128]{2,1,0:T(4,128)(2,1)S(1)}, bf16[72,4,128]{2,1,0:T(4,128)(2,1)S(1)}, u32[]{:S(2)}, u32[]{:S(2)}) collective-permute-start(bf16[72,4,128]{2,1,0:T(4,128)(2,1)S(1)} %get-tuple-element.75), channel_id=1, source_target_pairs={{0,1},{1,2},{2,3},{4,5},{5,6},{6,7},{8,9},{9,10},{10,11},{12,13},{... | collective-permute-start | bytes 221192 | tf_op jit(solution)/shard_map/ppermute | solution.py:19
  251.9 5.7 %collective-permute-start.15 = (bf16[72,4,128]{2,1,0:T(4,128)(2,1)S(1)}, bf16[72,4,128]{2,1,0:T(4,128)(2,1)S(1)}, u32[]{:S(2)}, u32[]{:S(2)}) collective-permute-start(bf16[72,4,128]{2,1,0:T(4,128)(2,1)S(1)} %get-tuple-element.76), channel_id=1, source_target_pairs={{1,0},{2,1},{3,2},{5,4},{6,5},{7,6},{9,8},{10,9},{11,10},{13,12},{... | collective-permute-start | bytes 221192 | tf_op jit(solution)/shard_map/ppermute | solution.py:21
  258.3 1.1 copy-start.6
  259.4 1.1 copy-start.4
  260.5 1.1 copy-start.2
  262.8 3.5 copy-start.15
  288.0 13.5 %collective-permute-start.16 = (bf16[4,4,64,128]{3,2,1,0:T(8,128)(2,1)S(1)}, bf16[4,4,64,128]{3,2,1,0:T(8,128)(2,1)S(1)}, u32[]{:S(2)}, u32[]{:S(2)}) collective-permute-start(bf16[4,4,64,128]{3,2,1,0:T(8,128)(2,1)S(1)} %get-tuple-element.69), channel_id=1, source_target_pairs={{0,4},{4,8},{8,12},{12,16},{16,20},{20,24},{24,28},{1,5},{5,9},{9,... | collective-permute-start | bytes 786440 | tf_op jit(solution)/shard_map/ppermute | solution.py:19
  289.9 11.6 %collective-permute-start.17 = (bf16[4,4,64,128]{3,2,1,0:T(8,128)(2,1)S(1)}, bf16[4,4,64,128]{3,2,1,0:T(8,128)(2,1)S(1)}, u32[]{:S(2)}, u32[]{:S(2)}) collective-permute-start(bf16[4,4,64,128]{3,2,1,0:T(8,128)(2,1)S(1)} %get-tuple-element.70), channel_id=1, source_target_pairs={{4,0},{8,4},{12,8},{16,12},{20,16},{24,20},{28,24},{5,1},{9,5},{13... | collective-permute-start | bytes 786440 | tf_op jit(solution)/shard_map/ppermute | solution.py:21
  301.7 5.6 %collective-permute-start.18 = (bf16[4,72,4,128]{3,2,1,0:T(4,128)(2,1)S(1)}, bf16[4,72,4,128]{3,2,1,0:T(4,128)(2,1)S(1)}, u32[]{:S(2)}, u32[]{:S(2)}) collective-permute-start(bf16[4,72,4,128]{3,2,1,0:T(4,128)(2,1)S(1)} %get-tuple-element.65), channel_id=1, source_target_pairs={{0,1},{1,2},{2,3},{4,5},{5,6},{6,7},{8,9},{9,10},{10,11},{12,13},{... | collective-permute-start | bytes 884744 | tf_op jit(solution)/shard_map/ppermute | solution.py:19
  303.7 8.0 %collective-permute-start.19 = (bf16[4,72,4,128]{3,2,1,0:T(4,128)(2,1)S(1)}, bf16[4,72,4,128]{3,2,1,0:T(4,128)(2,1)S(1)}, u32[]{:S(2)}, u32[]{:S(2)}) collective-permute-start(bf16[4,72,4,128]{3,2,1,0:T(4,128)(2,1)S(1)} %get-tuple-element.66), channel_id=1, source_target_pairs={{1,0},{2,1},{3,2},{5,4},{6,5},{7,6},{9,8},{10,9},{11,10},{13,12},{... | collective-permute-start | bytes 884744 | tf_op jit(solution)/shard_map/ppermute | solution.py:21
where the time goes:
time: 354 us; the launch traced here: 349 us
  matrix products  123 us (35%)
  waiting for transfers between devices  78 us (22%)
  starting transfers between devices  60.6 us (17%)
  other arithmetic  54.8 us (15%)
  local copies, waits for them, and re-layouts  21.3 us (6%)
  between operations  11.1 us (3%)
    dot_general x16, matrix products, blur_local(): jnp.einsum('ij,xjz->xiz', band_rows(taps_y, cols_out), first, precision=l...  56 us
    ppermute x10, waiting for transfers between devices, padded_2(): lax.ppermute(tail, axis, [(i, (i + 1) % count) for i in range(ends)])  42.5 us
    dot_general x16, matrix products, blur_local(): jnp.einsum('xyj,ji->xyi', second, depth_band(taps_z, field.shape[2]), pre...  41.7 us
    ppermute x10, starting transfers between devices, padded_2(): lax.ppermute(tail, axis, [(i, (i + 1) % count) for i in range(ends)])  32.8 us
    concatenate x4, other arithmetic, padded_2(): jnp.concatenate([lax.ppermute(tail, axis, [(i, (i + 1) % count) for i in...  32.3 us
    ppermute x10, waiting for transfers between devices, padded_2(): lax.ppermute(head, axis, [((i + 1) % count, i) for i in range(ends)])  26.6 us
    ppermute x10, starting transfers between devices, padded_2(): lax.ppermute(head, axis, [((i + 1) % count, i) for i in range(ends)])  21.6 us
    dot_general x16, matrix products, blur_local(): jnp.einsum('ij,jyz->iyz', band_rows(taps_x, rows_out), field, precision=l...  18.2 us
  transfers between devices with their start and end apart: 21, of which 15 were waited for; matrix products, arithmetic and copies ran while one was open for 18% of the time, Pallas kernels for 0%

commit v1 on v0

v1 whole, which is shorter than its diff:
```python
import functools
import jax
import jax.numpy as jnp
from jax import lax
from jax.experimental import pallas as pl
from jax.experimental.pallas import tpu as pltpu
from jax.sharding import PartitionSpec as P

V = 4
SHIFT = 16
ITERS = 2
H = 4
MESH = pl.DeviceIdType.MESH
F32 = jnp.float32
BF16 = jnp.bfloat16
WAYS = [(1, 0), (-1, 0), (0, 1), (0, -1), (1, 1), (1, -1), (-1, 1), (-1, -1)]


def both(*terms):
    out = terms[0]
    for term in terms[1:]:
        out = jnp.logical_and(out, term)
    return out


def greet(nbx, nby, partners):
    barrier = pltpu.get_barrier_semaphore()
    count = jnp.int32(0)
    for px, py, exists in partners:
        @pl.when(exists)
        def _():
            pl.semaphore_signal(barrier, inc=1, device_id=(px, py), device_id_type=MESH)

        count = count + jnp.where(exists, 1, 0)
    pl.semaphore_wait(barrier, count)


def register_kernel(nbx, nby, blk, rows_y, views, o0, o1, o2, o3, send, recv):
    bx = lax.axis_index("bx")
    by = lax.axis_index("by")
    s = SHIFT // blk
    outs = (o0, o1, o2, o3)
    low = (-s, 0, -s, s)
    count = (nby, nby + s, nby + s, nby)
    left = (-SHIFT, -SHIFT, 0, SHIFT)
    width = (rows_y, rows_y + SHIFT, rows_y + SHIFT, rows_y)
    full = nby * rows_y

    greet(
        nbx,
        nby,
        [
            (bx + dx, jnp.int32(to), both(bx + dx >= 0, bx + dx < nbx, jnp.logical_or(by != to, dx != 0)))
            for dx in (-1, 0, 1)
            for to in range(nby)
        ],
    )

    def columns(view, to):
        first = to * rows_y + left[view]
        begin, end = max(first, 0), min(first + width[view], full)
        return begin, begin - first, end - begin

    def each_send(act):
        for view in range(V):
            for slot, dx in enumerate((-1, 0, 1)):
                k = by - low[view] - nby * dx
                wanted = both(k >= 0, k < count[view], bx + dx >= 0, bx + dx < nbx)
                for step in range(nby):
                    for to in range(nby):
                        turn = lax.rem(by + 1 + step, nby) == to
                        act(view, slot, dx, k, to, both(wanted, turn))

    def start(view, slot, dx, k, to, cond):
        begin, at, wide = columns(view, to)

        def refs():
            row = pl.multiple_of(k * blk, blk)
            return (
                views.at[view, :, pl.ds(begin, wide), :],
                outs[view].at[pl.ds(row, blk), pl.ds(at, wide), :],
            )

        mine = by == to if dx == 0 else None

        @pl.when(cond if mine is None else both(cond, jnp.logical_not(mine)))
        def _():
            src, dst = refs()
            pltpu.make_async_remote_copy(
                src_ref=src,
                dst_ref=dst,
                send_sem=send.at[view, slot, to],
                recv_sem=recv.at[view, k],
                device_id=(bx + dx, jnp.int32(to)),
                device_id_type=MESH,
            ).start()

        if mine is not None:
            @pl.when(both(cond, mine))
            def _():
                src, dst = refs()
                pltpu.make_async_copy(src, dst, recv.at[view, k]).start()

    each_send(start)

    for view in range(V):
        for k in range(count[view]):
            source = nby * bx + low[view] + k
            for to in sorted({0, 1, nby - 1}):
                position = by == to if to in (0, nby - 1) else both(by > 0, by < nby - 1)
                _, at, wide = columns(view, to)

                @pl.when(both(position, source >= 0, source < nbx * nby))
                def _():
                    dst = outs[view].at[pl.ds(k * blk, blk), pl.ds(at, wide), :]
                    pltpu.make_async_copy(dst, dst, recv.at[view, k]).wait()

    for view in range(V):
        for slot, dx in enumerate((-1, 0, 1)):
            k = by - low[view] - nby * dx
            wanted = both(k >= 0, k < count[view], bx + dx >= 0, bx + dx < nbx)
            for to in range(nby):
                cond = both(wanted, by != to) if dx == 0 else wanted
                begin, _, wide = columns(view, to)

                @pl.when(cond)
                def _():
                    src = views.at[view, :, pl.ds(begin, wide), :]
                    pltpu.make_async_copy(src, src, send.at[view, slot, to]).wait()


def deconvolve_kernel(
    nbx, nby, nx, ny, est, reg, tx, ty, bg, wx, planes, band_f, band_t,
    out, E, R, T, U, S, pack, sx, sy, sc, gx, gy, gc, send, recv,
):
    bx = lax.axis_index("bx")
    by = lax.axis_index("by")
    taps = 2 * H + 1
    blocks = nx // 8

    def at(dx, dy):
        return both(bx + dx >= 0, bx + dx < nbx, by + dy >= 0, by + dy < nby)

    greet(nbx, nby, [(bx + dx, by + dy, at(dx, dy)) for dx, dy in WAYS])

    def clear(i, c):
        E[i] = jnp.zeros_like(E[i])
        for v in range(V):
            R[v, i] = jnp.zeros_like(R[v, i])
        return c

    lax.fori_loop(0, nx + 2 * H, clear, 0)

    def message(way, turn, which):
        dx, dy = WAYS[way]
        if dy == 0:
            mine, theirs, n = sx, gx, way
        elif dx == 0:
            mine, theirs, n = sy, gy, way - 2
        else:
            mine, theirs, n = sc, gc, way - 4
        return pltpu.make_async_remote_copy(
            src_ref=mine.at[turn, which, n],
            dst_ref=theirs.at[turn, which, n],
            send_sem=send.at[turn, which, way],
            recv_sem=recv.at[turn, which, way],
            device_id=(bx + dx, by + dy),
            device_id_type=MESH,
        )

    def offer(field, turn, which):
        for n, first in ((0, nx), (1, H)):
            for k in range(H):
                sx[turn, which, n, k * ny : (k + 1) * ny] = field[first + k, 8 : 8 + ny].astype(BF16)

        for n, first in ((0, ny + 8 - H), (1, 8)):
            def rim(i, c):
                for j in range(4):
                    pack[j * H : (j + 1) * H] = field[H + 4 * i + j, first : first + H]
                sy[turn, which, n, pl.ds(pl.multiple_of(16 * i, 16), 16)] = pack[...].astype(BF16)
                return c

            lax.fori_loop(0, nx // 4, rim, 0)
        for n, (dx, dy) in enumerate(WAYS[4:]):
            fx = nx if dx == 1 else H
            fy = ny + 8 - H if dy == 1 else 8
            for k in range(H):
                pack[k * H : (k + 1) * H] = field[fx + k, fy : fy + H]
            sc[turn, which, n] = pack[...].astype(BF16)
        for way, (dx, dy) in enumerate(WAYS):
            @pl.when(at(dx, dy))
            def _():
                message(way, turn, which).start()

    def accept(field, turn, which):
        for way, (dx, dy) in enumerate(WAYS):
            @pl.when(at(-dx, -dy))
            def _():
                message(way, turn, which).wait_recv()
                fx = 0 if dx == 1 else nx + H
                fy = 8 - H if dy == 1 else ny + 8
                if dy == 0:
                    for k in range(H):
                        field[fx + k, 8 : 8 + ny] = gx[turn, which, way, k * ny : (k + 1) * ny].astype(F32)
                elif dx == 0:
                    def rim(i, c):
                        rows = gy[turn, which, way - 2, pl.ds(pl.multiple_of(16 * i, 16), 16)].astype(F32)
                        for j in range(4):
                            field[H + 4 * i + j, fy : fy + H] = rows[j * H : (j + 1) * H]
                        return c

                    lax.fori_loop(0, nx // 4, rim, 0)
                else:
                    rows = gc[turn, which, way - 4].astype(F32)
                    for k in range(H):
                        field[fx + k, fy : fy + H] = rows[k * H : (k + 1) * H]

        for way, (dx, dy) in enumerate(WAYS):
            @pl.when(at(dx, dy))
            def _():
                message(way, turn, which).wait_send()

    def blurred(field, i, ax, ay, band):
        for t in range((ny + 2 * H) // 8):
            rows = [field[8 * i + k, 8 - H + 8 * t : 16 - H + 8 * t] for k in range(7 + taps)]
            for o in range(8):
                acc = ax[0] * rows[o]
                for a in range(1, taps):
                    acc = acc + ax[a] * rows[o + a]
                T[o, 8 * t : 8 * t + 8] = acc
        for o in range(8):
            for t in range(ny // 8):
                acc = ay[0] * T[o, 8 * t : 8 * t + 8]
                for b in range(1, taps):
                    acc = acc + ay[b] * T[o, 8 * t + b : 8 * t + b + 8]
                U[o * ny + 8 * t : o * ny + 8 * t + 8] = acc
        value = U[...]
        high = value.astype(BF16)
        rest = (value - high.astype(F32)).astype(BF16)
        return jnp.dot(
            jnp.concatenate([high, rest, high], axis=1), band, preferred_element_type=F32
        )

    def load(i, c):
        E[H + i, 8 : 8 + ny] = est[i]
        return c

    lax.fori_loop(0, nx, load, 0)

    def sweep(turn, c):
        offer(E, turn, V)
        accept(E, turn, V)

        def ahead(v, c):
            ax = [tx[v, a] for a in range(taps)]
            ay = [ty[v, a] for a in range(taps)]
            base = bg[v]

            def block(i, c):
                got = blurred(E, i, ax, ay, band_f[v])
                for o in range(8):
                    R[v, H + 8 * i + o, 8 : 8 + ny] = reg[v, 8 * i + o].astype(F32) / (
                        got[o * ny : (o + 1) * ny] + base
                    )
                return c

            lax.fori_loop(0, blocks, block, 0)
            offer(R.at[v], turn, v)
            return c

        lax.fori_loop(0, V, ahead, 0)

        def back(v, c):
            accept(R.at[v], turn, v)
            ax = [tx[v, taps - 1 - a] for a in range(taps)]
            ay = [ty[v, taps - 1 - a] for a in range(taps)]
            keep = jnp.where(v == 0, 0.0, 1.0).astype(F32)

            def block(i, c):
                got = blurred(R.at[v], i, ax, ay, band_t[v])
                for o in range(8):
                    S[8 * i + o] = S[8 * i + o] * keep + got[o * ny : (o + 1) * ny]
                return c

            lax.fori_loop(0, blocks, block, 0)
            return c

        def empty(i, c):
            S[i] = jnp.zeros_like(S[i])
            return c

        lax.fori_loop(0, nx, empty, 0)
        lax.fori_loop(0, V, back, 0)

        def update(i, c):
            weight = wx[0, i] * planes[0]
            for v in range(1, V):
                weight = weight + wx[v, i] * planes[v]
            E[H + i, 8 : 8 + ny] = E[H + i, 8 : 8 + ny] * S[i] / weight
            return c

        lax.fori_loop(0, nx, update, 0)
        return c

    lax.fori_loop(0, ITERS, sweep, 0)

    def store(i, c):
        out[i] = E[H + i, 8 : 8 + ny]
        return c

    lax.fori_loop(0, nx, store, 0)


def band_rows(tap_row, extent):
    length = tap_row.shape[0]
    distance = jnp.arange(extent + length - 1)[None, :] - jnp.arange(extent)[:, None]
    picked = distance[:, :, None] == jnp.arange(length)[None, None, :]
    return jnp.sum(jnp.where(picked, tap_row[None, None, :], 0.0), axis=2)


def depth_bands(taps, extent):
    length = taps.shape[1]
    middle = (length - 1) // 2
    distance = jnp.arange(extent)[:, None] - jnp.arange(extent)[None, :] + middle
    band = jnp.zeros((taps.shape[0], extent, extent), F32)
    for lag in range(length):
        band = jnp.where(distance[None] == lag, taps[:, lag, None, None], band)
    return band


def stacked(band):
    high = band.astype(BF16)
    rest = (band - high.astype(F32)).astype(BF16)
    return jnp.concatenate([high, high, rest], axis=1)


def local(views, offsets, background, psf_x, psf_y, psf_z, start):
    rows_x, rows_y, depth = start.shape
    nbx = lax.axis_size("bx")
    nby = lax.axis_size("by")
    full_x = rows_x * nbx
    full_y = rows_y * nby
    blk = views.shape[1]
    middle = (psf_x.shape[1] - 1) // 2
    spread = SHIFT // blk
    vmem = pl.BlockSpec(memory_space=pltpu.VMEM)
    smem = pl.BlockSpec(memory_space=pltpu.SMEM)
    anywhere = pl.BlockSpec(memory_space=pl.ANY)

    moved = pl.pallas_call(
        functools.partial(register_kernel, nbx, nby, blk, rows_y),
        out_shape=[
            jax.ShapeDtypeStruct((rows_x, rows_y, depth), BF16),
            jax.ShapeDtypeStruct((rows_x + SHIFT, rows_y + SHIFT, depth), BF16),
            jax.ShapeDtypeStruct((rows_x + SHIFT, rows_y + SHIFT, depth), BF16),
            jax.ShapeDtypeStruct((rows_x, rows_y, depth), BF16),
        ],
        in_specs=[anywhere],
        out_specs=[anywhere] * 4,
        scratch_shapes=[
            pltpu.SemaphoreType.DMA((V, 3, nby)),
            pltpu.SemaphoreType.DMA((V, nby + spread)),
        ],
        compiler_params=pltpu.CompilerParams(collective_id=0, has_side_effects=True),
    )(views)

    taps_x = psf_x / jnp.sum(psf_x, axis=1, keepdims=True)
    taps_y = psf_y / jnp.sum(psf_y, axis=1, keepdims=True)
    taps_z = psf_z / jnp.sum(psf_z, axis=1, keepdims=True)
    at_x = lax.axis_index("bx") * rows_x - middle + jnp.arange(rows_x + 2 * middle, dtype=jnp.int32)
    at_y = lax.axis_index("by") * rows_y - middle + jnp.arange(rows_y + 2 * middle, dtype=jnp.int32)

    def covered(at, shift, full):
        there = at[None, :] + shift[:, None]
        return (at >= 0) & (at < full) & (there >= 0) & (there < full)

    cover_x = covered(at_x, offsets[:, 0], full_x)
    cover_y = covered(at_y, offsets[:, 1], full_y)

    def folded(cover, taps, rows):
        total = jnp.zeros((V, rows), F32)
        for lag in range(2 * middle + 1):
            total = total + taps[:, 2 * middle - lag, None] * cover[:, lag : lag + rows].astype(F32)
        return total

    weight_x = folded(cover_x, taps_x, rows_x)
    weight_y = folded(cover_y, taps_y, rows_y)
    band_f = depth_bands(taps_z, depth)
    band_t = depth_bands(taps_z[:, ::-1], depth)
    weight_z = jnp.sum(band_t, axis=1)
    planes = weight_y[:, :, None] * weight_z[:, None, :]

    zero = jnp.zeros((), jnp.int32)
    size = (rows_x, rows_y, depth)
    cut = [
        moved[0],
        lax.dynamic_slice(moved[1], (offsets[1, 0], SHIFT + offsets[1, 1], zero), size),
        lax.dynamic_slice(moved[2], (SHIFT + offsets[2, 0], offsets[2, 1], zero), size),
        moved[3],
    ]
    inner_x = cover_x[:, middle : middle + rows_x]
    inner_y = cover_y[:, middle : middle + rows_y]
    registered = jnp.stack(
        [
            jnp.where(inner_x[v][:, None, None] & inner_y[v][None, :, None], cut[v], jnp.zeros((), BF16))
            for v in range(V)
        ]
    )

    rim_x = H * rows_y
    rim_y = H * rows_x
    return pl.pallas_call(
        functools.partial(deconvolve_kernel, nbx, nby, rows_x, rows_y),
        out_shape=jax.ShapeDtypeStruct(start.shape, F32),
        in_specs=[vmem, vmem, smem, smem, smem, smem, vmem, vmem, vmem],
        out_specs=vmem,
        scratch_shapes=[
            pltpu.VMEM((rows_x + 2 * H, rows_y + 16, depth), F32),
            pltpu.VMEM((V, rows_x + 2 * H, rows_y + 16, depth), F32),
            pltpu.VMEM((8, rows_y + 2 * H, depth), F32),
            pltpu.VMEM((8 * rows_y, depth), F32),
            pltpu.VMEM(start.shape, F32),
            pltpu.VMEM((16, depth), F32),
            pltpu.VMEM((ITERS, V + 1, 2, rim_x, depth), BF16),
            pltpu.VMEM((ITERS, V + 1, 2, rim_y, depth), BF16),
            pltpu.VMEM((ITERS, V + 1, 4, 16, depth), BF16),
            pltpu.VMEM((ITERS, V + 1, 2, rim_x, depth), BF16),
            pltpu.VMEM((ITERS, V + 1, 2, rim_y, depth), BF16),
            pltpu.VMEM((ITERS, V + 1, 4, 16, depth), BF16),
            pltpu.SemaphoreType.DMA((ITERS, V + 1, 8)),
            pltpu.SemaphoreType.DMA((ITERS, V + 1, 8)),
        ],
        compiler_params=pltpu.CompilerParams(
            collective_id=1, has_side_effects=True, vmem_limit_bytes=56 * 1024 * 1024
        ),
    )(start, registered, taps_x, taps_y, background, weight_x, planes, stacked(band_f), stacked(band_t))


def solution(mesh):
    return jax.shard_map(
        local,
        mesh=mesh,
        in_specs=(P(None, ("bx", "by"), None, None), P(), P(), P(), P(), P(), P("bx", "by", None)),
        out_specs=P("bx", "by", None),
        check_vma=False,
    )
```

time: 354 us -> 194 us (0.55); the launches traced: 349 us -> 193 us
  Pallas kernels: 0 us -> 165 us
  matrix products: 123 us -> 0 us
  waiting for transfers between devices: 78 us -> 0 us
  starting transfers between devices: 60.6 us -> 0 us
  other arithmetic: 54.8 us -> 14.5 us
  local copies, waits for them, and re-layouts: 21.3 us -> 6.96 us
  between operations: 11.1 us -> 6.83 us
    pallas_call x0 -> x2, Pallas kernels: none -> 165 us  [the longest x1 111 us: local(): pl.pallas_call(functools.partial(deconvolve_kernel, nbx, nby, rows_x, row...]
    dot_general x56 -> x0, matrix products: 123 us -> none  [the longest x16 56 us: blur_local(): jnp.einsum('ij,xjz->xiz', band_rows(taps_y, cols_out), first, precision=l...]
    ppermute x20 -> x0, waiting for transfers between devices: 69.1 us -> none  [the longest x10 42.5 us: padded_2(): lax.ppermute(tail, axis, [(i, (i + 1) % count) for i in range(ends)])]
    ppermute x20 -> x0, starting transfers between devices: 54.4 us -> none  [the longest x10 32.8 us: padded_2(): lax.ppermute(tail, axis, [(i, (i + 1) % count) for i in range(ends)])]
    concatenate x4 -> x2, other arithmetic: 32.3 us -> 1.61 us  [stacked(): return jnp.concatenate([high, high, rest], axis=1)]
    all_to_all x1 -> x0, waiting for transfers between devices: 8.95 us -> none  [local(): lax.all_to_all(views, 'by', split_axis=2, concat_axis=1, tiled=True)]
    another operation x0 -> x3, other arithmetic: none -> 8.58 us  [local(): jnp.stack([jnp.where(inner_x[v][:, None, None] & inner_y[v][None, :, None...]
    div x3 -> x2, other arithmetic: 8.13 us -> 0.15 us  [the longest x1 0.08 us: local(): taps_y = psf_y / jnp.sum(psf_y, axis=1, keepdims=True)]
  transfers between devices with their start and end apart: 21 -> 0, of which waited for: 15 -> 0; matrix products, arithmetic and copies ran while one was open for 18% -> 0% of each run, Pallas kernels for 0% -> 0%
where the time goes in v1:
time: 194 us; the launch traced here: 193 us
  Pallas kernels  165 us (85%)
  other arithmetic  14.5 us (7%)
  local copies, waits for them, and re-layouts  6.96 us (4%)
  between operations  6.83 us (4%)
    pallas_call x1, Pallas kernels, local(): pl.pallas_call(functools.partial(deconvolve_kernel, nbx, nby, rows_x, row...  111 us
    pallas_call x1, Pallas kernels, local(): pl.pallas_call(functools.partial(register_kernel, nbx, nby, blk, rows_y),...  54.1 us
    another operation x3, other arithmetic, local(): jnp.stack([jnp.where(inner_x[v][:, None, None] & inner_y[v][None, :, None...  8.58 us

profile of v1, /device:TPU:5, one launch (start us, length us, event | category | flops | bytes accessed | tf_op | source)
XLA Modules:
  0.0 193.4 jit_solution(10584006273498068716)
XLA Ops:
  0.0 0.8 slice_bitcast_fusion.9
  0.8 0.1 fusion.22
  0.9 0.1 slice_bitcast_fusion.7
  1.0 0.1 fusion.24
  1.0 0.1 slice_bitcast_fusion.6
  1.1 0.1 broadcast_and_fusion.2
  1.2 0.1 broadcast_and_fusion.3
  1.3 1.5 fusion.25
  6.2 54.1 %shard_map.73 = (bf16[64,64,128]{2,1,0:T(8,128)(2,1)}, bf16[80,80,128]{2,1,0:T(8,128)(2,1)}, bf16[80,80,128]{2,1,0:T(8,128)(2,1)}, bf16[64,64,128]{2,1,0:T(8,128)(2,1)}) custom-call(bf16[4,16,256,128]{3,2,1,0:T(8,128)(2,1)} %views.1), custom_call_target="tpu_custom_call" | custom-call | tf_op jit(solution)/shard_map/pallas_call | solution.py:350
  60.3 0.0 copy-start
  60.3 3.3 %select_bitcast_fusion.2 = (bf16[1,64,64,128]{3,2,1,0:T(8,128)(2,1)S(1)}, bf16[1,64,64,128]{3,2,1,0:T(8,128)(2,1)S(1)}) fusion(bf16[80,80,128]{2,1,0:T(8,128)(2,1)} %get-tuple-element.10, s32[]{:T(128)S(6)} %select_n.153, s32[]{:T(128)S(6)} %select_n.154, pred[64,64]{1,0:T(8,128)(4,1)S(1)} %broadcast_and_fusion.2, bf16[64,64,128]{2,1,0:T(8,128)(2,1)} %get-tuple-element.9, ...), kind=kLoop, calls=%fused_computation.3 | loop fusion | flops 1048576 | bytes 4202504 | tf_op jit(solution)/shard_map/stack | solution.py:403
  63.6 0.1 broadcast_and_fusion
  63.7 0.1 broadcast_and_fusion.1
  67.0 0.0 copy-done
  67.0 3.0 %select_bitcast_fusion = (bf16[1,64,64,128]{3,2,1,0:T(8,128)(2,1)S(1)}, bf16[1,64,64,128]{3,2,1,0:T(8,128)(2,1)S(1)}) fusion(bf16[64,64,128]{2,1,0:T(8,128)(2,1)S(1)} %copy-done, pred[64,64]{1,0:T(8,128)(4,1)S(1)} %broadcast_and_fusion, bf16[80,80,128]{2,1,0:T(8,128)(2,1)} %get-tuple-element.11, s32[]{:T(128)S(6)} %select_n.156, s32[]{:T(128)S(6)} %select_n.157, ...), kind=kLoop, calls=%fused_computation.1 | loop fusion | flops 1048576 | bytes 4202504 | tf_op jit(solution)/shard_map/stack | solution.py:403
  70.1 0.0 copy-start.3
  70.1 0.0 copy-start.5
  70.1 0.0 copy-start.4
  70.1 2.2 %pad_maximum_fusion.reg = bf16[4,64,64,128]{3,2,1,0:T(8,128)(2,1)} fusion(bf16[1,64,64,128]{3,2,1,0:T(8,128)(2,1)S(1)} %get-tuple-element.71, bf16[1,64,64,128]{3,2,1,0:T(8,128)(2,1)S(1)} %get-tuple-element.72, bf16[1,64,64,128]{3,2,1,0:T(8,128)(2,1)S(1)} %get-tuple-element.73, bf16[1,64,64,128]{3,2,1,0:T(8,128)(2,1)S(1)} %get-tuple-element.74), kind=kLoop, calls=%fused_computation | loop fusion | flops 6291456 | bytes 8388608 | tf_op jit(solution)/shard_map/stack | solution.py:403
  72.3 0.0 copy-done.3
  72.3 0.1 reduce_sum.38
  72.5 0.1 broadcast_divide_fusion
  72.5 0.5 slice_reduce_fusion.20
  73.0 0.2 slice_reduce_fusion.19
  73.6 0.7 subtract_convert_fusion
  74.4 0.8 pad_maximum_fusion.2.band_t
  75.2 0.7 subtract_convert_fusion.1
  75.9 0.8 pad_maximum_fusion.1.band_f
  76.7 0.0 copy-done.5
  76.7 0.1 reduce_sum.36
  76.9 0.0 copy-done.4
  76.9 0.1 reduce_sum.37
  77.0 0.1 broadcast_divide_fusion.1
  77.1 0.0 copy-start.1
  77.1 0.0 copy-start.2
  77.1 0.3 slice_reduce_fusion.29
  77.4 0.1 select_add_fusion
  77.5 0.8 broadcast_multiply_fusion.planes
  78.2 0.3 slice_reduce_fusion.38
  78.6 0.7 select_add_fusion.1.wx
  79.2 0.0 copy-done.1
  79.2 0.0 copy-done.2
  79.2 111.0 %shard_map.74 = f32[64,64,128]{2,1,0:T(8,128)} custom-call(f32[64,64,128]{2,1,0:T(8,128)} %est.1, bf16[4,64,64,128]{3,2,1,0:T(8,128)(2,1)} %pad_maximum_fusion.reg, f32[4,9]{1,0:T(4,128)} %copy-done.2, f32[4,9]{1,0:T(4,128)} %copy-done.1, f32[4]{0:T(128)} %bg.1, f32[4,64]{1,0:T(4,128)} %select_add_fusion.1.wx, f32[4,64,128]{2,1,0:T(8,128)} %broadcast_multiply_fusion.planes, ...), custom_call_target="tpu_custom_call" | custom-call | tf_op jit(solution)/shard_map/pallas_call | solution.py:412
  190.2 3.2 %copy.9 = f32[64,64,128]{2,1,0:T(8,128)} copy(f32[64,64,128]{2,1,0:T(8,128)} %shard_map.74) | data formatting | bytes 4194304
  (16 shorter events, 0.4 us)
Async XLA Ops:
  60.3 6.7 %copy-start = (bf16[64,64,128]{2,1,0:T(8,128)(2,1)S(1)}, bf16[64,64,128]{2,1,0:T(8,128)(2,1)}, u32[]{:S(2)}) copy-start(bf16[64,64,128]{2,1,0:T(8,128)(2,1)} %get-tuple-element.12) | copy-start | bytes 3145732
  70.1 2.3 %copy-start.3 = (f32[4,21]{1,0:T(4,128)S(1)}, f32[4,21]{1,0:T(4,128)}, u32[]{:S(2)}) copy-start(f32[4,21]{1,0:T(4,128)} %param.12) | copy-start | bytes 1012
  70.1 6.7 %copy-start.5 = (f32[4,9]{1,0:T(4,128)S(1)}, f32[4,9]{1,0:T(4,128)}, u32[]{:S(2)}) copy-start(f32[4,9]{1,0:T(4,128)} %param.10) | copy-start | bytes 436
  70.1 6.8 %copy-start.4 = (f32[4,9]{1,0:T(4,128)S(1)}, f32[4,9]{1,0:T(4,128)}, u32[]{:S(2)}) copy-start(f32[4,9]{1,0:T(4,128)} %param.11) | copy-start | bytes 436
  77.1 2.2 %copy-start.1 = (f32[4,9]{1,0:T(4,128)}, f32[4,9]{1,0:T(4,128)S(1)}, u32[]{:S(2)}) copy-start(f32[4,9]{1,0:T(4,128)S(1)} %get-tuple-element.95.ty) | copy-start | bytes 436
  77.1 2.2 %copy-start.2 = (f32[4,9]{1,0:T(4,128)}, f32[4,9]{1,0:T(4,128)S(1)}, u32[]{:S(2)}) copy-start(f32[4,9]{1,0:T(4,128)S(1)} %get-tuple-element.96.tx) | copy-start | bytes 436

commit v2 on v0

v2 whole, which is shorter than its diff:
```python
import functools
import jax
import jax.numpy as jnp
from jax import lax
from jax.experimental import pallas as pl
from jax.experimental.pallas import tpu as pltpu
from jax.sharding import PartitionSpec as P

V = 4
SHIFT = 16
ITERS = 2
H = 4
MESH = pl.DeviceIdType.MESH
F32 = jnp.float32
BF16 = jnp.bfloat16
WAYS = [(1, 0), (-1, 0), (0, 1), (0, -1), (1, 1), (1, -1), (-1, 1), (-1, -1)]


def both(*terms):
    out = terms[0]
    for term in terms[1:]:
        out = jnp.logical_and(out, term)
    return out


def greet(nbx, nby, partners):
    barrier = pltpu.get_barrier_semaphore()
    count = jnp.int32(0)
    for px, py, exists in partners:
        @pl.when(exists)
        def _():
            pl.semaphore_signal(barrier, inc=1, device_id=(px, py), device_id_type=MESH)

        count = count + jnp.where(exists, 1, 0)
    pl.semaphore_wait(barrier, count)


def deconvolve_kernel(
    nbx, nby, nx, ny, blk, depth,
    views, start, taps, offsets, bg,
    out, r0, r1, r2, r3, E, inverse, Eb, Rb, halo, rim, G, U, ratio, pack, LF, LT, ZF, ZT, pick, planes, WX,
    send_v, recv_v, send, recv,
):
    bx = lax.axis_index("bx")
    by = lax.axis_index("by")
    kxy = 2 * H + 1
    kz = taps.shape[1] - 2 * kxy
    blocks = nx // 8
    s = SHIFT // blk
    regs = (r0, r1, r2, r3)
    low = (-s, 0, -s, s)
    count = (nby, nby + s, nby + s, nby)
    left = (-SHIFT, -SHIFT, 0, SHIFT)
    width = (ny, ny + SHIFT, ny + SHIFT, ny)
    full = nby * ny

    def at(dx, dy):
        return both(bx + dx >= 0, bx + dx < nbx, by + dy >= 0, by + dy < nby)

    def columns(view, to):
        first = to * ny + left[view]
        begin, end = max(first, 0), min(first + width[view], full)
        return begin, begin - first, end - begin

    def row_block(view, dx):
        k = by - low[view] - nby * dx
        return k, both(k >= 0, k < count[view], bx + dx >= 0, bx + dx < nbx)

    def start_view(view, slot, dx, k, to, cond):
        begin, at_y, wide = columns(view, to)

        def refs():
            row = pl.multiple_of(k * blk, blk)
            return (
                views.at[view, :, pl.ds(begin, wide), :],
                regs[view].at[pl.ds(row, blk), pl.ds(at_y, wide), :],
            )

        mine = by == to if dx == 0 else None

        @pl.when(cond if mine is None else both(cond, jnp.logical_not(mine)))
        def _():
            src, dst = refs()
            pltpu.make_async_remote_copy(
                src_ref=src,
                dst_ref=dst,
                send_sem=send_v.at[view, slot, to],
                recv_sem=recv_v.at[view, k],
                device_id=(bx + dx, jnp.int32(to)),
                device_id_type=MESH,
            ).start()

        if mine is not None:
            @pl.when(both(cond, mine))
            def _():
                src, dst = refs()
                pltpu.make_async_copy(src, dst, recv_v.at[view, k]).start()

    def start_views():
        for view in range(V):
            for slot, dx in enumerate((-1, 0, 1)):
                k, wanted = row_block(view, dx)
                for step in range(nby):
                    for to in range(nby):
                        turn = lax.rem(by + 1 + step, nby) == to
                        start_view(view, slot, dx, k, to, both(wanted, turn))

    def accept_view(view):
        for k in range(count[view]):
            source = nby * bx + low[view] + k
            for to in sorted({0, 1, nby - 1}):
                position = by == to if to in (0, nby - 1) else both(by > 0, by < nby - 1)
                _, at_y, wide = columns(view, to)

                @pl.when(both(position, source >= 0, source < nbx * nby))
                def _():
                    dst = regs[view].at[pl.ds(k * blk, blk), pl.ds(at_y, wide), :]
                    pltpu.make_async_copy(dst, dst, recv_v.at[view, k]).wait()

    def finish_views():
        for view in range(V):
            for slot, dx in enumerate((-1, 0, 1)):
                k, wanted = row_block(view, dx)
                for to in range(nby):
                    begin, _, wide = columns(view, to)

                    @pl.when(both(wanted, by != to) if dx == 0 else wanted)
                    def _():
                        src = views.at[view, :, pl.ds(begin, wide), :]
                        pltpu.make_async_copy(src, src, send_v.at[view, slot, to]).wait()

    def message(field, turn, which, way):
        dx, dy = WAYS[way]
        side = 0 if dy == 1 else 1
        if dy == 0:
            src = field.at[pl.ds(nx if dx == 1 else H, H)]
            dst = field.at[pl.ds(0 if dx == 1 else nx + H, H)]
        elif dx == 0:
            src = rim.at[turn, which, side]
            dst = halo.at[turn, which, side, pl.ds(16, 4 * nx)]
        else:
            src = rim.at[turn, which, side, pl.ds(4 * nx - 16 if dx == 1 else 0, 16)]
            dst = halo.at[turn, which, side, pl.ds(0 if dx == 1 else 4 * nx + 16, 16)]
        return pltpu.make_async_remote_copy(
            src_ref=src,
            dst_ref=dst,
            send_sem=send.at[turn, which, way],
            recv_sem=recv.at[turn, which, way],
            device_id=(bx + dx, by + dy),
            device_id_type=MESH,
        )

    def offer(field, turn, which):
        for way, (dx, dy) in enumerate(WAYS):
            @pl.when(at(dx, dy))
            def _():
                message(field, turn, which, way).start()

    def accept(field, turn, which):
        for way, (dx, dy) in enumerate(WAYS):
            @pl.when(at(-dx, -dy))
            def _():
                message(field, turn, which, way).wait_recv()

    def finish(field, turn, which):
        for way, (dx, dy) in enumerate(WAYS):
            @pl.when(at(dx, dy))
            def _():
                message(field, turn, which, way).wait_send()

    def pack_rim(source, turn, which, i):
        for o in range(8):
            row = source(o)
            pack[0, o * H : (o + 1) * H] = row[ny - H : ny]
            pack[1, o * H : (o + 1) * H] = row[0:H]
        for side in range(2):
            rim[turn, which, side, pl.ds(pl.multiple_of(32 * i, 32), 32)] = pack[side].astype(BF16)

    def publish(turn):
        def block(i, c):
            for o in range(8):
                Eb[turn, H + 8 * i + o] = E[8 * i + o].astype(BF16)
            pack_rim(lambda o: E.at[8 * i + o], turn, V, i)
            return c

        lax.fori_loop(0, blocks, block, 0)

    def clear_small(i, c):
        r0[i] = jnp.zeros((ny, depth), BF16)
        r3[i] = jnp.zeros((ny, depth), BF16)
        E[i] = start[i]
        return c

    def clear_large(i, c):
        r1[i] = jnp.zeros((ny + SHIFT, depth), BF16)
        r2[i] = jnp.zeros((ny + SHIFT, depth), BF16)
        return c

    lax.fori_loop(0, nx, clear_small, 0)
    lax.fori_loop(0, nx + SHIFT, clear_large, 0)
    for turn in range(ITERS):
        for k in range(H):
            for first in (0, nx + H):
                Eb[turn, first + k] = jnp.zeros((ny, depth), BF16)
                for v in range(V):
                    Rb[turn, v, first + k] = jnp.zeros((ny, depth), BF16)

        def clear_halo(which, c):
            for side in range(2):
                halo[turn, which, side] = jnp.zeros((4 * nx + 32, depth), BF16)
            return c

        lax.fori_loop(0, V + 1, clear_halo, 0)
    publish(0)

    greet(
        nbx,
        nby,
        [
            (bx + dx, jnp.int32(to), both(bx + dx >= 0, bx + dx < nbx, jnp.logical_or(by != to, dx != 0)))
            for dx in (-1, 0, 1)
            for to in range(nby)
        ],
    )
    offer(Eb.at[0], 0, V)
    start_views()

    def split(band):
        high = band.astype(BF16)
        return high, (band - high.astype(F32)).astype(BF16)

    row = lax.broadcasted_iota(jnp.int32, (ny, 128), 0)
    col = lax.broadcasted_iota(jnp.int32, (ny, 128), 1)
    inside = col < ny
    second = col >= ny + 16
    place = jnp.where(inside, col, jnp.where(second, ny + (col & 3), (col & 3) - H))
    owner = jnp.where(inside, -1, (col & 15) >> 2)
    lag_y = place - row + H
    z_in = lax.broadcasted_iota(jnp.int32, (depth, depth), 0)
    z_out = lax.broadcasted_iota(jnp.int32, (depth, depth), 1)
    lag_z = z_in - z_out + (kz - 1) // 2

    def build(v, c):
        forth = jnp.zeros((ny, 128), F32)
        back = jnp.zeros((ny, 128), F32)
        for b in range(kxy):
            forth = jnp.where(lag_y == b, taps[v, kxy + b], forth)
            back = jnp.where(lag_y == b, taps[v, 2 * kxy - 1 - b], back)
        for j in range(4):
            used = jnp.logical_and(
                jnp.logical_or(owner == -1, owner == j), col < ny + 32
            )
            for side, (target, band) in enumerate(((LF, forth), (LT, back))):
                high, rest = split(jnp.where(used, band, 0.0))
                base = pl.multiple_of(v * ny, ny)
                target[j, pl.ds(base, ny), 0:128] = high
                target[j, pl.ds(base, ny), 128:256] = rest
        forth = jnp.zeros((depth, depth), F32)
        back = jnp.zeros((depth, depth), F32)
        for b in range(kz):
            forth = jnp.where(lag_z == b, taps[v, 2 * kxy + b], forth)
            back = jnp.where(lag_z == b, taps[v, 2 * kxy + kz - 1 - b], back)
        for target, band in ((ZF, forth), (ZT, back)):
            high, rest = split(band)
            base = pl.multiple_of(v * 3 * depth, 3 * depth)
            target[pl.ds(base, depth)] = high
            target[pl.ds(base + depth, depth)] = high
            target[pl.ds(base + 2 * depth, depth)] = rest
        weight_z = jnp.sum(back, axis=0, keepdims=True)

        def folded(first, shift, limit, base, rows):
            total = jnp.zeros((rows, 128), F32)
            cell = first - H + lax.broadcasted_iota(jnp.int32, (rows, 128), 0)
            for b in range(kxy):
                here = cell + b
                there = here + shift
                good = both(here >= 0, here < limit, there >= 0, there < limit)
                total = total + jnp.where(good, taps[v, base + kxy - 1 - b], 0.0)
            return total

        planes[v] = folded(by * ny, offsets[v, 1], nby * ny, kxy, ny) * weight_z
        WX[v] = folded(bx * nx, offsets[v, 0], nbx * nx, 0, nx)
        return c

    lax.fori_loop(0, V, build, 0)

    pick_row = lax.broadcasted_iota(jnp.int32, (ny, ny + SHIFT), 0)
    pick_col = lax.broadcasted_iota(jnp.int32, (ny, ny + SHIFT), 1)
    for n, shift in enumerate((SHIFT + offsets[1, 1], offsets[2, 1])):
        pick[n] = jnp.where(pick_col == pick_row + shift, 1.0, 0.0).astype(BF16)

    def invert(i, c):
        rows = [WX[v, pl.ds(pl.multiple_of(8 * i, 8), 8)] for v in range(V)]
        for o in range(8):
            weight = rows[0][o : o + 1] * planes[0]
            for v in range(1, V):
                weight = weight + rows[v][o : o + 1] * planes[v]
            inverse[8 * i + o] = 1.0 / weight
        return c

    lax.fori_loop(0, blocks, invert, 0)

    def column(field, turn, which, q, j):
        tile = pl.ds(pl.multiple_of(16 * q, 16), 16)
        once = [
            field[4 * q + j],
            halo[turn, which, 0, tile],
            halo[turn, which, 1, tile],
            jnp.zeros((128 - ny - 32, depth), BF16),
        ]
        return jnp.concatenate(once + once, axis=0)

    def along_x(v, i, reverse):
        weights = [taps[v, kxy - 1 - a if reverse else a] for a in range(kxy)]
        for t in range(0, ny, 16):
            halves = []
            for u in (t, t + 8):
                rows = [G[v, 8 * i + k, u : u + 8] for k in range(7 + kxy)]
                sums = []
                for o in range(8):
                    acc = weights[0] * rows[o]
                    for a in range(1, kxy):
                        acc = acc + weights[a] * rows[o + a]
                    sums.append(acc)
                halves.append(sums)
            for o in range(8):
                both_halves = jnp.concatenate([halves[0][o], halves[1][o]], axis=0)
                high, rest = split(both_halves)
                U[v, o * ny + t : o * ny + t + 16, :depth] = high
                U[v, o * ny + t : o * ny + t + 16, depth:] = rest

    def sweep(turn, c):
        accept(Eb.at[turn], turn, V)

        def all_views(q, c):
            for j in range(4):
                got = jnp.dot(
                    LF[j], column(Eb.at[turn], turn, V, q, j), preferred_element_type=F32
                )
                for v in range(V):
                    G[v, 4 * q + j] = got[v * ny : (v + 1) * ny]
            return c

        lax.fori_loop(0, (nx + 2 * H) // 4, all_views, 0)

        for v in range(V):
            @pl.when(turn == 0)
            def _():
                accept_view(v)

            first_x = {1: offsets[1, 0], 2: SHIFT + offsets[2, 0]}.get(v, 0)

            def ahead(i, c):
                along_x(v, i, False)
                got = jnp.dot(
                    jnp.concatenate([U[v], U[v, :, :depth]], axis=1),
                    ZF[3 * v * depth : 3 * (v + 1) * depth],
                    preferred_element_type=F32,
                )
                for o in range(8):
                    if v in (1, 2):
                        seen = jnp.dot(
                            pick[v - 1], regs[v][first_x + 8 * i + o], preferred_element_type=F32
                        )
                    else:
                        seen = regs[v][8 * i + o].astype(F32)
                    value = seen / (got[o * ny : (o + 1) * ny] + bg[v])
                    Rb[turn, v, H + 8 * i + o] = value.astype(BF16)
                    ratio[o] = value
                pack_rim(lambda o: ratio.at[o], turn, v, i)
                return c

            lax.fori_loop(0, blocks, ahead, 0)
            offer(Rb.at[turn, v], turn, v)

        def back(v, c):
            accept(Rb.at[turn, v], turn, v)

            def one_view(q, c):
                for j in range(4):
                    G[v, 4 * q + j] = jnp.dot(
                        LT[j, pl.ds(pl.multiple_of(v * ny, ny), ny)],
                        column(Rb.at[turn, v], turn, v, q, j),
                        preferred_element_type=F32,
                    )
                return c

            lax.fori_loop(0, (nx + 2 * H) // 4, one_view, 0)
            return c

        lax.fori_loop(0, V, back, 0)

        def update(i, c):
            for v in range(V):
                along_x(v, i, True)
            got = jnp.dot(
                jnp.concatenate(
                    [part for v in range(V) for part in (U[v], U[v, :, :depth])], axis=1
                ),
                ZT[...],
                preferred_element_type=F32,
            )
            for o in range(8):
                x = 8 * i + o
                E[x] = E[x] * got[o * ny : (o + 1) * ny] * inverse[x]
            return c

        lax.fori_loop(0, blocks, update, 0)

        finish(Eb.at[turn], turn, V)
        for v in range(V):
            finish(Rb.at[turn, v], turn, v)

        @pl.when(turn < ITERS - 1)
        def _():
            publish(turn + 1)
            offer(Eb.at[turn + 1], turn + 1, V)

        return c

    lax.fori_loop(0, ITERS, sweep, 0)
    finish_views()

    def store(i, c):
        out[i] = E[i]
        return c

    lax.fori_loop(0, nx, store, 0)


def local(views, offsets, background, psf_x, psf_y, psf_z, start):
    rows_x, rows_y, depth = start.shape
    nbx = lax.axis_size("bx")
    nby = lax.axis_size("by")
    blk = views.shape[1]
    vmem = pl.BlockSpec(memory_space=pltpu.VMEM)
    smem = pl.BlockSpec(memory_space=pltpu.SMEM)
    anywhere = pl.BlockSpec(memory_space=pl.ANY)
    taps = jnp.concatenate([p / jnp.sum(p, axis=1, keepdims=True) for p in (psf_x, psf_y, psf_z)], axis=1)
    tall = rows_x + 2 * H
    small = (rows_x, rows_y, depth)
    large = (rows_x + SHIFT, rows_y + SHIFT, depth)
    return pl.pallas_call(
        functools.partial(deconvolve_kernel, nbx, nby, rows_x, rows_y, blk, depth),
        out_shape=jax.ShapeDtypeStruct(start.shape, F32),
        in_specs=[anywhere, vmem, smem, smem, smem],
        out_specs=vmem,
        scratch_shapes=[
            pltpu.VMEM(small, BF16),
            pltpu.VMEM(large, BF16),
            pltpu.VMEM(large, BF16),
            pltpu.VMEM(small, BF16),
            pltpu.VMEM(small, F32),
            pltpu.VMEM(small, F32),
            pltpu.VMEM((ITERS, tall, rows_y, depth), BF16),
            pltpu.VMEM((ITERS, V, tall, rows_y, depth), BF16),
            pltpu.VMEM((ITERS, V + 1, 2, H * tall, depth), BF16),
            pltpu.VMEM((ITERS, V + 1, 2, H * rows_x, depth), BF16),
            pltpu.VMEM((V, tall, rows_y, depth), F32),
            pltpu.VMEM((V, 8 * rows_y, 2 * depth), BF16),
            pltpu.VMEM((8, rows_y, depth), F32),
            pltpu.VMEM((2, 32, depth), F32),
            pltpu.VMEM((4, V * rows_y, 256), BF16),
            pltpu.VMEM((4, V * rows_y, 256), BF16),
            pltpu.VMEM((3 * V * depth, depth), BF16),
            pltpu.VMEM((3 * V * depth, depth), BF16),
            pltpu.VMEM((2, rows_y, rows_y + SHIFT), BF16),
            pltpu.VMEM((V, rows_y, depth), F32),
            pltpu.VMEM((V, rows_x, depth), F32),
            pltpu.SemaphoreType.DMA((V, 3, nby)),
            pltpu.SemaphoreType.DMA((V, nby + SHIFT // blk)),
            pltpu.SemaphoreType.DMA((ITERS, V + 1, 8)),
            pltpu.SemaphoreType.DMA((ITERS, V + 1, 8)),
        ],
        compiler_params=pltpu.CompilerParams(
            collective_id=0, has_side_effects=True, vmem_limit_bytes=56 * 1024 * 1024
        ),
    )(views, start, taps, offsets, background)


def solution(mesh):
    return jax.shard_map(
        local,
        mesh=mesh,
        in_specs=(P(None, ("bx", "by"), None, None), P(), P(), P(), P(), P(), P("bx", "by", None)),
        out_specs=P("bx", "by", None),
        check_vma=False,
    )
```

time: 354 us -> 154 us (0.44)
  Pallas kernels: 0 us -> 142 us
  matrix products: 123 us -> 0 us
  waiting for transfers between devices: 78 us -> 0 us
  starting transfers between devices: 60.6 us -> 0 us
  other arithmetic: 54.8 us -> 4.58 us
  local copies, waits for them, and re-layouts: 21.3 us -> 4.52 us
  between operations: 11.1 us -> 0.01 us
    pallas_call x0 -> x1, Pallas kernels: none -> 142 us  [local(): pl.pallas_call(functools.partial(deconvolve_kernel, nbx, nby, rows_x, row...]
    dot_general x56 -> x0, matrix products: 123 us -> none  [the longest x16 56 us: blur_local(): jnp.einsum('ij,xjz->xiz', band_rows(taps_y, cols_out), first, precision=l...]
    ppermute x20 -> x0, waiting for transfers between devices: 69.1 us -> none  [the longest x10 42.5 us: padded_2(): lax.ppermute(tail, axis, [(i, (i + 1) % count) for i in range(ends)])]
    ppermute x20 -> x0, starting transfers between devices: 54.4 us -> none  [the longest x10 32.8 us: padded_2(): lax.ppermute(tail, axis, [(i, (i + 1) % count) for i in range(ends)])]
    concatenate x4 -> x1, other arithmetic: 32.3 us -> 0.66 us  [local(): jnp.concatenate([p / jnp.sum(p, axis=1, keepdims=True) for p in (psf_x, p...]
    all_to_all x1 -> x0, waiting for transfers between devices: 8.95 us -> none  [local(): lax.all_to_all(views, 'by', split_axis=2, concat_axis=1, tiled=True)]
    div x3 -> x2, other arithmetic: 8.13 us -> 1.52 us  [local(): p / jnp.sum(p, axis=1, keepdims=True)]
    all_to_all x1 -> x0, starting transfers between devices: 6.19 us -> none  [local(): lax.all_to_all(views, 'by', split_axis=2, concat_axis=1, tiled=True)]
  transfers between devices with their start and end apart: 21 -> 0, of which waited for: 15 -> 0; matrix products, arithmetic and copies ran while one was open for 18% -> 0% of each run, Pallas kernels for 0% -> 0%
where the time goes in v2:
time: 154 us; the launch traced here: 151 us
  Pallas kernels  142 us (92%)
  other arithmetic  4.58 us (3%)
  local copies, waits for them, and re-layouts  4.52 us (3%)
    pallas_call x1, Pallas kernels, local(): pl.pallas_call(functools.partial(deconvolve_kernel, nbx, nby, rows_x, row...  142 us
    unnamed x2, local copies, waits for them, and re-layouts  4.52 us

profile of v2, /device:TPU:5, one launch (start us, length us, event | category | flops | bytes accessed | tf_op | source)
XLA Modules:
  0.0 151.1 jit_solution(13528666268983718307)
XLA Ops:
  0.0 0.8 reduce_sum.27
  0.8 0.8 reduce_sum.28
  1.6 0.8 reduce_sum.29
  2.4 0.8 broadcast_divide_fusion
  3.2 1.4 copy.8.offsets
  4.5 0.8 broadcast_divide_fusion.1
  5.3 0.7 pad_maximum_fusion.taps
  5.9 142.0 %shard_map.73 = f32[64,64,128]{2,1,0:T(8,128)} custom-call(bf16[4,16,256,128]{3,2,1,0:T(8,128)(2,1)} %views.1, f32[64,64,128]{2,1,0:T(8,128)} %start.1, f32[4,39]{1,0:T(4,128)} %pad_maximum_fusion.taps, s32[4,2]{1,0:T(4,128)} %copy.8.offsets, f32[4]{0:T(128)} %bg.1), custom_call_target="tpu_custom_call" | custom-call | tf_op jit(solution)/shard_map/pallas_call | solution.py:443
  148.0 3.2 %copy.10 = f32[64,64,128]{2,1,0:T(8,128)} copy(f32[64,64,128]{2,1,0:T(8,128)} %shard_map.73) | data formatting | bytes 4194304

commit v3 on v2

--- a/solution.py
+++ b/solution.py
@@ -38,7 +38,7 @@
 def deconvolve_kernel(
     nbx, nby, nx, ny, blk, depth,
     views, start, taps, offsets, bg,
-    out, r0, r1, r2, r3, E, inverse, Eb, Rb, halo, rim, G, U, ratio, pack, LF, LT, ZF, ZT, pick, planes, WX,
+    out, r0, r1, r2, r3, E, inverse, Eb, Rb, halo, rim, G, U, D, ratio, pack, LF, LT, ZF, ZT, pick, planes, WX,
     send_v, recv_v, send, recv,
 ):
     bx = lax.axis_index("bx")
@@ -240,7 +240,15 @@
     z_out = lax.broadcasted_iota(jnp.int32, (depth, depth), 1)
     lag_z = z_in - z_out + (kz - 1) // 2
 
+    def total_of(v, first, length):
+        total = taps[v, first]
+        for b in range(1, length):
+            total = total + taps[v, first + b]
+        return total
+
     def build(v, c):
+        scale_xy = 1.0 / jnp.full((ny, 128), total_of(v, 0, kxy) * total_of(v, kxy, kxy), F32)
+        scale_z = 1.0 / jnp.full((depth, depth), total_of(v, 2 * kxy, kz), F32)
         forth = jnp.zeros((ny, 128), F32)
         back = jnp.zeros((ny, 128), F32)
         for b in range(kxy):
@@ -250,8 +258,8 @@
             used = jnp.logical_and(
                 jnp.logical_or(owner == -1, owner == j), col < ny + 32
             )
-            for side, (target, band) in enumerate(((LF, forth), (LT, back))):
-                high, rest = split(jnp.where(used, band, 0.0))
+            for target, band in ((LF, forth), (LT, back)):
+                high, rest = split(jnp.where(used, band * scale_xy, 0.0))
                 base = pl.multiple_of(v * ny, ny)
                 target[j, pl.ds(base, ny), 0:128] = high
                 target[j, pl.ds(base, ny), 128:256] = rest
@@ -260,6 +268,8 @@
         for b in range(kz):
             forth = jnp.where(lag_z == b, taps[v, 2 * kxy + b], forth)
             back = jnp.where(lag_z == b, taps[v, 2 * kxy + kz - 1 - b], back)
+        forth = forth * scale_z
+        back = back * scale_z
         for target, band in ((ZF, forth), (ZT, back)):
             high, rest = split(band)
             base = pl.multiple_of(v * 3 * depth, 3 * depth)
@@ -278,7 +288,7 @@
                 total = total + jnp.where(good, taps[v, base + kxy - 1 - b], 0.0)
             return total
 
-        planes[v] = folded(by * ny, offsets[v, 1], nby * ny, kxy, ny) * weight_z
+        planes[v] = folded(by * ny, offsets[v, 1], nby * ny, kxy, ny) * scale_xy * weight_z
         WX[v] = folded(bx * nx, offsets[v, 0], nbx * nx, 0, nx)
         return c
 
@@ -310,7 +320,7 @@
         ]
         return jnp.concatenate(once + once, axis=0)
 
-    def along_x(v, i, reverse):
+    def along_x(v, i, reverse, base):
         weights = [taps[v, kxy - 1 - a if reverse else a] for a in range(kxy)]
         for t in range(0, ny, 16):
             halves = []
@@ -326,8 +336,8 @@
             for o in range(8):
                 both_halves = jnp.concatenate([halves[0][o], halves[1][o]], axis=0)
                 high, rest = split(both_halves)
-                U[v, o * ny + t : o * ny + t + 16, :depth] = high
-                U[v, o * ny + t : o * ny + t + 16, depth:] = rest
+                U[v, pl.ds(base + o * ny + t, 16), :depth] = high
+                U[v, pl.ds(base + o * ny + t, 16), depth:] = rest
 
     def sweep(turn, c):
         accept(Eb.at[turn], turn, V)
@@ -343,20 +353,47 @@
 
         lax.fori_loop(0, (nx + 2 * H) // 4, all_views, 0)
 
+        def back(v):
+            accept(Rb.at[turn, v], turn, v)
+
+            def one_view(q, c):
+                for j in range(4):
+                    G[v, 4 * q + j] = jnp.dot(
+                        LT[j, v * ny : (v + 1) * ny],
+                        column(Rb.at[turn, v], turn, v, q, j),
+                        preferred_element_type=F32,
+                    )
+                return c
+
+            lax.fori_loop(0, (nx + 2 * H) // 4, one_view, 0)
+
+            def block(i, c):
+                along_x(v, i, True, pl.multiple_of(8 * ny * i, 8 * ny))
+                return c
+
+            lax.fori_loop(0, blocks, block, 0)
+
         for v in range(V):
+            first_x = {1: offsets[1, 0], 2: SHIFT + offsets[2, 0]}.get(v, 0)
+
+            def ahead(i, c):
+                along_x(v, i, False, 0)
+                got = jnp.dot(
+                    jnp.concatenate([U[v, : 8 * ny], U[v, : 8 * ny, :depth]], axis=1),
+                    ZF[3 * v * depth : 3 * (v + 1) * depth],
+                    preferred_element_type=F32,
+                )
+                for o in range(8):
+                    D[8 * i + o] = got[o * ny : (o + 1) * ny] + bg[v]
+                return c
+
+            lax.fori_loop(0, blocks, ahead, 0)
+
             @pl.when(turn == 0)
             def _():
                 accept_view(v)
 
-            first_x = {1: offsets[1, 0], 2: SHIFT + offsets[2, 0]}.get(v, 0)
-
-            def ahead(i, c):
-                along_x(v, i, False)
-                got = jnp.dot(
-                    jnp.concatenate([U[v], U[v, :, :depth]], axis=1),
-                    ZF[3 * v * depth : 3 * (v + 1) * depth],
-                    preferred_element_type=F32,
-                )
+            def divide(i, c):
                 for o in range(8):
                     if v in (1, 2):
                         seen = jnp.dot(
@@ -364,38 +401,23 @@
                         )
                     else:
                         seen = regs[v][8 * i + o].astype(F32)
-                    value = seen / (got[o * ny : (o + 1) * ny] + bg[v])
+                    value = seen / D[8 * i + o]
                     Rb[turn, v, H + 8 * i + o] = value.astype(BF16)
                     ratio[o] = value
                 pack_rim(lambda o: ratio.at[o], turn, v, i)
                 return c
 
-            lax.fori_loop(0, blocks, ahead, 0)
+            lax.fori_loop(0, blocks, divide, 0)
             offer(Rb.at[turn, v], turn, v)
-
-        def back(v, c):
-            accept(Rb.at[turn, v], turn, v)
-
-            def one_view(q, c):
-                for j in range(4):
-                    G[v, 4 * q + j] = jnp.dot(
-                        LT[j, pl.ds(pl.multiple_of(v * ny, ny), ny)],
-                        column(Rb.at[turn, v], turn, v, q, j),
-                        preferred_element_type=F32,
-                    )
-                return c
-
-            lax.fori_loop(0, (nx + 2 * H) // 4, one_view, 0)
-            return c
-
-        lax.fori_loop(0, V, back, 0)
+            if v:
+                back(v - 1)
+        back(V - 1)
 
         def update(i, c):
-            for v in range(V):
-                along_x(v, i, True)
+            here = pl.ds(pl.multiple_of(8 * ny * i, 8 * ny), 8 * ny)
             got = jnp.dot(
                 jnp.concatenate(
-                    [part for v in range(V) for part in (U[v], U[v, :, :depth])], axis=1
+                    [part for v in range(V) for part in (U[v, here], U[v, here, :depth])], axis=1
                 ),
                 ZT[...],
                 preferred_element_type=F32,
@@ -436,7 +458,7 @@
     vmem = pl.BlockSpec(memory_space=pltpu.VMEM)
     smem = pl.BlockSpec(memory_space=pltpu.SMEM)
     anywhere = pl.BlockSpec(memory_space=pl.ANY)
-    taps = jnp.concatenate([p / jnp.sum(p, axis=1, keepdims=True) for p in (psf_x, psf_y, psf_z)], axis=1)
+    taps = jnp.concatenate([psf_x, psf_y, psf_z], axis=1)
     tall = rows_x + 2 * H
     small = (rows_x, rows_y, depth)
     large = (rows_x + SHIFT, rows_y + SHIFT, depth)
@@ -457,7 +479,8 @@
             pltpu.VMEM((ITERS, V + 1, 2, H * tall, depth), BF16),
             pltpu.VMEM((ITERS, V + 1, 2, H * rows_x, depth), BF16),
             pltpu.VMEM((V, tall, rows_y, depth), F32),
-            pltpu.VMEM((V, 8 * rows_y, 2 * depth), BF16),
+            pltpu.VMEM((V, rows_x * rows_y, 2 * depth), BF16),
+            pltpu.VMEM(small, F32),
             pltpu.VMEM((8, rows_y, depth), F32),
             pltpu.VMEM((2, 32, depth), F32),
             pltpu.VMEM((4, V * rows_y, 256), BF16),
@@ -473,7 +496,7 @@
             pltpu.SemaphoreType.DMA((ITERS, V + 1, 8)),
         ],
         compiler_params=pltpu.CompilerParams(
-            collective_id=0, has_side_effects=True, vmem_limit_bytes=56 * 1024 * 1024
+            collective_id=0, has_side_effects=True, vmem_limit_bytes=60 * 1024 * 1024
         ),
     )(views, start, taps, offsets, background)
 

time: 154 us -> 159 us (1.032); the launches traced: 151 us -> 159 us
  Pallas kernels: 142 us -> 153 us
  other arithmetic: 4.58 us -> 1.37 us
    pallas_call x1, Pallas kernels: 142 us -> 153 us  [local(): pl.pallas_call(functools.partial(deconvolve_kernel, nbx, nby, rows_x, row...]
    reduce_sum x3 -> x0, other arithmetic: 2.4 us -> none  [local(): jnp.sum(p, axis=1, keepdims=True)]
where the time goes in v3:
time: 159 us
  Pallas kernels  153 us (96%)
  local copies, waits for them, and re-layouts  4.51 us (3%)
    pallas_call x1, Pallas kernels, local(): pl.pallas_call(functools.partial(deconvolve_kernel, nbx, nby, rows_x, row...  153 us
    unnamed x2, local copies, waits for them, and re-layouts  4.51 us

profile of v3, /device:TPU:5, one launch (start us, length us, event | category | flops | bytes accessed | tf_op | source)
XLA Modules:
  0.0 158.5 jit_solution(13176928069720197596)
XLA Ops:
  0.0 1.4 copy.8.offsets
  1.4 1.4 pad_maximum_fusion.taps
  2.7 152.6 %shard_map.73 = f32[64,64,128]{2,1,0:T(8,128)} custom-call(bf16[4,16,256,128]{3,2,1,0:T(8,128)(2,1)} %views.1, f32[64,64,128]{2,1,0:T(8,128)} %start.1, f32[4,39]{1,0:T(4,128)} %pad_maximum_fusion.taps, s32[4,2]{1,0:T(4,128)} %copy.8.offsets, f32[4]{0:T(128)} %bg.1), custom_call_target="tpu_custom_call" | custom-call | tf_op jit(solution)/shard_map/pallas_call | solution.py:465
  155.4 3.2 %copy.10 = f32[64,64,128]{2,1,0:T(8,128)} copy(f32[64,64,128]{2,1,0:T(8,128)} %shard_map.73) | data formatting | bytes 4194304
